TPU v7x, 256 devices: a whole 4x4x8 slice. The times are simulated.
256 devices in a mesh: tensor: 8 (over z_hi, y), replica: 32 (over x, z_lo, core).
Axes of the slice: x: 4, y: 4, z: 8 (z_hi: 2, z_lo: 4; z = z_hi * 4 + z_lo), core: 2. Of those that a mesh axis runs over, the one named last changes fastest.
Arguments:
- tokens: bfloat16 [10240, 6144], P('replica', 'tensor'), may hold values from -6 to 6
- cotangent: bfloat16 [10240, 1024], P('replica', 'tensor'), may hold values from -6 to 6
- weights: bfloat16 [6144, 1024], P(None, 'tensor'), may hold values from -0.078125 to 0.078125
- momentum: float32 [32, 6144, 1024], P('replica', None, 'tensor'), may hold values from -6 to 6
Outputs:
- input_grad: bfloat16 [10240, 6144], P('replica', 'tensor')
- momentum_out: float32 [32, 6144, 1024], P('replica', None, 'tensor')
- update: float32 [6144, 1024], P(None, 'tensor')
All inputs are finite; a program needn't handle non-finite values.
Results may differ from a plain program's by a relative error of at most 0.015.
Values may be sent and summed in bfloat16 or wider, within the bound.
A program may use at most 128 MiB of HBM per device.

v0:
```python
import math

import jax
import jax.numpy as jnp
from jax import lax
from jax.sharding import PartitionSpec as P

SPAN = 64
KEEP = 16


decay_rate = 0.9


def cosine_table():
    order = jnp.arange(KEEP, dtype=jnp.float32)[:, None]
    place = jnp.arange(SPAN, dtype=jnp.float32)[None, :]
    table = jnp.cos(jnp.pi * (place + 0.5) * order / SPAN) * math.sqrt(2.0 / SPAN)
    return jnp.where(order == 0, table * math.sqrt(0.5), table)


def per_device(tokens, cotangent, weights, momentum):
    table = cosine_table()
    rows_full = lax.all_gather(tokens, "tensor", axis=1, tiled=True)
    depth = rows_full.shape[1]
    width = weights.shape[1]
    hidden = jnp.dot(rows_full, weights, preferred_element_type=jnp.float32)
    sig = jax.nn.sigmoid(hidden)
    grad_act = (cotangent.astype(jnp.float32) * sig * (1.0 + hidden * (1.0 - sig))).astype(
        jnp.bfloat16
    )
    partial_terms = lax.dot_general(
        grad_act, weights, (((1,), (1,)), ((), ())), preferred_element_type=jnp.float32
    )
    input_grad = lax.psum_scatter(
        partial_terms.astype(jnp.bfloat16), "tensor", scatter_dimension=1, tiled=True
    )
    grad_w = lax.dot_general(
        rows_full, grad_act, (((0,), (0,)), ((), ())), preferred_element_type=jnp.float32
    ) / math.sqrt(rows_full.shape[0])
    moment_new = decay_rate * momentum[0] + grad_w
    blocks = moment_new.reshape(depth // SPAN, SPAN, width)
    coeffs = jnp.einsum("kj,cjf->ckf", table, blocks, precision=lax.Precision.HIGHEST)
    rest = blocks - jnp.einsum("kj,ckf->cjf", table, coeffs, precision=lax.Precision.HIGHEST)
    sent = coeffs.astype(jnp.bfloat16)
    replicas = lax.axis_size("replica")
    total = jnp.sum(
        lax.all_gather(sent[None], "replica", axis=0, tiled=True).astype(jnp.float32), axis=0
    )
    update = jnp.einsum("kj,ckf->cjf", table, total, precision=lax.Precision.HIGHEST).reshape(
        depth, width
    ) / math.sqrt(replicas)
    return (input_grad, rest.reshape(1, depth, width), update)


def solution(mesh):
    in_specs = (
        P("replica", "tensor"),
        P("replica", "tensor"),
        P(None, "tensor"),
        P("replica", None, "tensor"),
    )
    out_specs = (P("replica", "tensor"), P("replica", None, "tensor"), P(None, "tensor"))
    return jax.shard_map(
        per_device, mesh=mesh, in_specs=in_specs, out_specs=out_specs, check_vma=False
    )
```

profile of v0, /device:TPU:1, one launch (start us, length us, event | category | flops | bytes accessed | tf_op | source)
XLA Modules:
  0.0 341.2 jit_solution(5435625592220196748)
XLA Ops:
  7.2 0.0 copy-start
  7.2 0.0 all-gather.4.cloned.1.call-start
  7.2 0.7 all-gather.4.cloned.1.call-update
  7.9 0.0 all-gather.6.cloned.1.call-start
  8.0 3.5 %copy.12 = f32[1,6144,128]{1,2,0:T(8,128)} copy(f32[1,6144,128]{2,1,0:T(8,128)} %param.7) | data formatting | bytes 6291456 | tf_op args[3]
  11.5 0.0 copy-start.2
  11.5 102.0 %all-gather.4.cloned.1.call-done = bf16[320,6144]{1,0:T(8,128)(2,1)} async-done(((bf16[320,768]{1,0:T(8,128)(2,1)}), bf16[320,6144]{1,0:T(8,128)(2,1)}) %all-gather.4.cloned.1.call-update) | async-done | bytes 3932176 | tf_op jit(solution)/shard_map/all_gather | solution.py:24
  113.5 0.0 copy-done
  113.5 0.0 copy-start.1
  113.5 3.4 %fusion.36 = f32[320,128]{1,0:T(8,128)S(1)} fusion(bf16[320,6144]{1,0:T(8,128)(2,1)} %all-gather.4.cloned.1.call-done, bf16[6144,128]{1,0:T(8,128)(2,1)S(1)} %copy-done), kind=kOutput, calls=%fused_computation.46 | convolution fusion | flops 503316480 | bytes 5668864 | tf_op jit(solution)/shard_map/dot_general | solution.py:27
  117.0 0.0 copy-done.2
  117.0 0.0 copy-done.1
  117.0 4.9 %fusion.1 = f32[6144,128]{0,1:T(8,128)} fusion(bf16[320,6144]{1,0:T(8,128)(2,1)S(1)} %copy-done.1, f32[1,6144,128]{1,2,0:T(8,128)} %copy.12, f32[320,128]{1,0:T(8,128)S(1)} %fusion.36, bf16[320,128]{1,0:T(8,128)(2,1)S(1)} %copy-done.2), kind=kOutput, calls=%fused_computation.4 | convolution fusion | flops 506085376 | bytes 10469376 | tf_op jit(solution)/shard_map/dot_general | solution.py:38
  121.9 3.5 %copy.13 = f32[6144,128]{1,0:T(8,128)} copy(f32[6144,128]{0,1:T(8,128)} %fusion.1) | data formatting | bytes 6291456 | tf_op jit(solution)/shard_map/add | solution.py:41
  125.4 4.4 %fusion.35 = (bf16[96,16,128]{2,1,0:T(8,128)(2,1)}, f32[96,16,128]{2,1,0:T(8,128)S(1)}) fusion(f32[96,64,128]{2,1,0:T(8,128)} %bitcast.33, f32[64]{0:T(128)S(1)} %add_multiply_fusion, pred[16]{0:T(512)(128)(4,1)S(1)} %iota_compare_fusion), kind=kOutput, calls=%fused_computation.45 | convolution fusion | flops 151196672 | bytes 4325648 | tf_op jit(solution)/shard_map/kj,cjf->ckf/dot_general | solution.py:43
  129.8 0.0 all-gather.6.cloned.1.call-update
  129.8 0.0 reduce-scatter.2.cloned.1.call-start
  129.9 3.1 convolution_convert_fusion
  132.9 0.0 reduce-scatter.2.cloned.1.call-update
  133.0 5.6 %bitcast_subtract_fusion = f32[96,64,128]{2,1,0:T(8,128)} fusion(f32[96,64,128]{2,1,0:T(8,128)} %bitcast.34, f32[96,16,128]{2,1,0:T(8,128)S(1)} %get-tuple-element.4, f32[64]{0:T(128)S(1)} %add_multiply_fusion, pred[16]{0:T(512)(128)(4,1)S(1)} %iota_compare_fusion), kind=kOutput, calls=%fused_computation.5 | convolution fusion | flops 151786496 | bytes 7078160 | tf_op jit(solution)/shard_map/kj,ckf->cjf/dot_general | solution.py:44
  138.5 69.7 %all-gather.6.cloned.1.call-done = bf16[3072,16,128]{2,1,0:T(8,128)(2,1)} async-done(((bf16[96,16,128]{2,1,0:T(8,128)(2,1)}), bf16[3072,16,128]{2,1,0:T(8,128)(2,1)}) %all-gather.6.cloned.1.call-update) | async-done | bytes 12582928 | tf_op jit(solution)/shard_map/all_gather | solution.py:48
  208.2 6.6 %convert_reduce_fusion = f32[96,16,128]{2,1,0:T(8,128)S(1)} fusion(bf16[32,96,16,128]{3,2,1,0:T(8,128)(2,1)} %bitcast.35), kind=kLoop, calls=%fused_computation | loop fusion | flops 12386304 | bytes 13369344 | tf_op jit(solution)/shard_map/reduce_sum | solution.py:47
  214.9 4.4 %convolution_multiply_fusion.1 = f32[96,128,64]{1,2,0:T(8,128)} fusion(f32[96,16,128]{2,1,0:T(8,128)S(1)} %convert_reduce_fusion, f32[64]{0:T(128)S(1)} %add_multiply_fusion, pred[16]{0:T(512)(128)(4,1)S(1)} %iota_compare_fusion), kind=kOutput, calls=%fused_computation.6 | convolution fusion | flops 151786496 | bytes 3932432 | tf_op jit(solution)/shard_map/kj,ckf->cjf/dot_general | solution.py:50
  219.3 115.4 %reduce-scatter.2.cloned.1.call-done = bf16[320,768]{1,0:T(8,128)(2,1)} async-done(((bf16[320,6144]{1,0:T(8,128)(2,1)}), bf16[320,768]{1,0:T(8,128)(2,1)}) %reduce-scatter.2.cloned.1.call-update) | async-done | bytes 491536 | tf_op jit(solution)/shard_map/reduce_scatter | solution.py:35
  (2 shorter events, 0.0 us)
Async XLA Ops:
  7.2 106.4 %copy-start = (bf16[6144,128]{1,0:T(8,128)(2,1)S(1)}, bf16[6144,128]{1,0:T(8,128)(2,1)}, u32[]{:S(2)}) copy-start(bf16[6144,128]{1,0:T(8,128)(2,1)} %param.6) | copy-start | bytes 4718596
  7.2 106.4 %all-gather.4.cloned.1.call-start = ((), (), s32[]{:S(2)}) async-start(), calls=%async_computation.1 | async-start | bytes 4423680 | tf_op jit(solution)/shard_map/all_gather | solution.py:24
  7.9 200.3 %all-gather.6.cloned.1.call-start = ((), (), s32[]{:S(2)}) async-start(), calls=%async_computation.3 | async-start | bytes 12976128 | tf_op jit(solution)/shard_map/all_gather | solution.py:48
  11.5 105.5 %copy-start.2 = (bf16[320,128]{1,0:T(8,128)(2,1)S(1)}, bf16[320,128]{1,0:T(8,128)(2,1)}, u32[]{:S(2)}) copy-start(bf16[320,128]{1,0:T(8,128)(2,1)} %param.5) | copy-start | bytes 245764
  113.5 3.5 %copy-start.1 = (bf16[320,6144]{1,0:T(8,128)(2,1)S(1)}, bf16[320,6144]{1,0:T(8,128)(2,1)}, u32[]{:S(2)}) copy-start(bf16[320,6144]{1,0:T(8,128)(2,1)} %all-gather.4.cloned.1.call-done) | copy-start | bytes 11796484
  129.8 204.8 %reduce-scatter.2.cloned.1.call-start = ((), (), s32[]{:S(2)}) async-start(), calls=%async_computation.2 | async-start | bytes 4423680 | tf_op jit(solution)/shard_map/reduce_scatter | solution.py:35
Sparse Core Ops, SparseCore 0:
  10.6 102.8 all-gather.3
  130.0 78.2 all-gather.5
  213.1 121.5 reduce-scatter.1
where the time goes:
time: 342 us; the launch traced here: 341 us
  waiting for transfers between devices  288 us (84%)
  matrix products  25.7 us (8%)
  between operations  13.8 us (4%)
  local copies, waits for them, and re-layouts  7.1 us (2%)
  other arithmetic  6.65 us (2%)
    reduce_scatter x1, waiting for transfers between devices, per_device(): lax.psum_scatter(partial_terms.astype(jnp.bfloat16), 'tensor', scatter_di...  115 us
    all_gather x1, waiting for transfers between devices, per_device(): rows_full = lax.all_gather(tokens, 'tensor', axis=1, tiled=True)  102 us
    all_gather x1, waiting for transfers between devices, per_device(): lax.all_gather(sent[None], 'replica', axis=0, tiled=True)  69.7 us
  transfers between devices with their start and end apart: 3, of which 3 were waited for; matrix products, arithmetic and copies ran while one was open for 7% of the time, Pallas kernels for 0%

commit v1 on v0

v1 whole, which is shorter than its diff:
```python
import math

import jax
import jax.numpy as jnp
import numpy as np
from jax import lax
from jax.experimental import pallas as pl
from jax.experimental.pallas import tpu as pltpu
from jax.sharding import PartitionSpec as P

SPAN = 64
KEEP = 16
D = 6144
TOK = 320
COLS = 768
WIDTH = 128
CODED = 192
CHUNK = 256
DECAY = 0.9
MESH = pl.DeviceIdType.MESH
F32 = jnp.float32
BF16 = jnp.bfloat16


def cosine_table():
    order = np.arange(KEEP, dtype=np.float64)[:, None]
    place = np.arange(SPAN, dtype=np.float64)[None, :]
    table = np.cos(np.pi * (place + 0.5) * order / SPAN) * math.sqrt(2.0 / SPAN)
    return np.where(order == 0, table * math.sqrt(0.5), table)


def coder():
    table = cosine_table()
    four = np.eye(CHUNK // SPAN)
    rest = np.kron(four, np.eye(SPAN) - table.T @ table)
    return np.concatenate([rest, np.kron(four, table)], axis=0)


def decoder():
    return np.kron(np.eye(CHUNK // SPAN), cosine_table().T)


def position():
    t = lax.axis_index("tensor")
    r = lax.axis_index("replica")
    return r // 8, t % 4, t // 4, (r // 2) % 4, r % 2


def device(x, y, zh, zl, c):
    return (zh * 4 + y, (x * 4 + zl) * 2 + c)


def step_kernel(
    tok_h, cot_ref, w_h, mom_h, coder_ref,
    grad_out, mom_out, tot_out,
    gathered, w_v, mom_v, high_t, low_t, low_pre, hidden, act, w_rows,
    own, from_core, from_x, from_z, part_x, part_z, total,
    send, recv, local,
):
    x, y, zh, zl, c = position()
    yr, yl, yo = (y + 1) % 4, (y + 3) % 4, (y + 2) % 4
    zo = 1 - zh
    right, left, opp = device(x, yr, zh, zl, c), device(x, yl, zh, zl, c), device(x, yo, zh, zl, c)
    far = device(x, y, zo, zl, c)
    far_l, far_r, far_o = device(x, yl, zo, zl, c), device(x, yr, zo, zl, c), device(x, yo, zo, zl, c)
    sibling = device(x, y, zh, zl, 1 - c)
    xs = [(x + d) % 4 for d in (1, 2, 3)]
    zs = [(zl + d) % 4 for d in (1, 2, 3)]
    x_peers = [device(v, y, zh, zl, c) for v in xs]
    z_peers = [device(x, y, zh, v, c) for v in zs]
    shard = [zh * 4 + v for v in (y, yl, yr, yo)] + [zo * 4 + v for v in (y, yl, yr, yo)]
    tensor_peers = [None, left, right, opp, far, far_l, far_r, far_o]

    counter = iter(range(1000))

    def remote(src, dst, target):
        k = next(counter)
        return pltpu.make_async_remote_copy(
            src_ref=src, dst_ref=dst, send_sem=send.at[k], recv_sem=recv.at[k],
            device_id=target, device_id_type=MESH,
        )

    barrier = pltpu.get_barrier_semaphore()
    partners = tensor_peers[1:] + [sibling] + x_peers + z_peers
    for p in partners:
        pl.semaphore_signal(barrier, inc=1, device_id=p, device_id_type=MESH)

    tok_in = pltpu.make_async_copy(tok_h, gathered.at[0], local.at[0])
    tok_in.start()
    w_in = pltpu.make_async_copy(w_h, w_v, local.at[1])
    w_in.start()
    mom_in = pltpu.make_async_copy(mom_h, mom_v, local.at[2])
    mom_in.start()
    hidden[...] = jnp.zeros_like(hidden)

    pl.semaphore_wait(barrier, len(partners))

    outgoing = []

    def go(copy):
        copy.start()
        outgoing.append(copy)
        return copy

    half = TOK // 2
    piece = 64
    pieces = TOK // piece
    far_in = []
    first = pl.ds(0, half)
    second = pl.ds(half, half)
    far_in.append(go(remote(tok_h.at[pl.ds(0, piece)], gathered.at[4, pl.ds(0, piece)], far)))
    from_l1 = go(remote(tok_h.at[first], gathered.at[1, first], right))
    from_r2 = go(remote(tok_h.at[second], gathered.at[2, second], left))
    for i in range(1, pieces):
        rows = pl.ds(i * piece, piece)
        far_in.append(go(remote(tok_h.at[rows], gathered.at[4, rows], far)))
    from_l2 = go(remote(tok_h.at[second], gathered.at[1, second], right))
    from_r1 = go(remote(tok_h.at[first], gathered.at[2, first], left))

    w_in.wait()
    w_copies = []
    mirror = [0, 2, 1, 3, 4, 6, 5, 7]
    share = 2 * x + c
    for s in range(1, 8):
        rows = pl.ds(pl.multiple_of(shard[s] * COLS + share * 96, 32), 96)
        w_copies.append(
            go(remote(w_v.at[rows], w_rows.at[mirror[s], share], tensor_peers[s]))
        )

    def process(slot):
        rows = pl.ds(pl.multiple_of(shard[slot] * COLS, COLS), COLS)
        hidden[...] += jnp.dot(gathered[slot], w_v[rows, :], preferred_element_type=F32)
        for j in range(COLS // CHUNK):
            coded = lax.dot_general(
                coder_ref[...], gathered[slot, :, j * CHUNK:(j + 1) * CHUNK],
                (((1,), (1,)), ((), ())), preferred_element_type=F32,
            ).astype(BF16)
            high_t[pl.ds(slot * COLS + j * CHUNK, CHUNK), :] = coded[:CHUNK]
            low_t[pl.ds(slot * CODED + j * SPAN, SPAN), :] = coded[CHUNK:]

    def momentum_pre(slot):
        def chunk(j, carry):
            rows = pl.ds(pl.multiple_of(shard[slot] * COLS + j * CHUNK, CHUNK), CHUNK)
            coded = DECAY * jnp.dot(
                coder_ref[...], mom_v[rows, :].astype(BF16), preferred_element_type=F32
            )
            mom_v[rows, :] = coded[:CHUNK]
            low_pre[pl.ds(pl.multiple_of(slot * CODED + j * SPAN, SPAN), SPAN), :] = coded[CHUNK:]
            return carry
        lax.fori_loop(0, COLS // CHUNK, chunk, 0)

    tok_in.wait()
    process(0)
    mom_in.wait()
    for s in range(3):
        momentum_pre(s)

    far_fwd_r, far_fwd_l, far_opp = [], [], []

    def forward_far(i):
        rows = pl.ds(i * piece, piece)
        far_in[i].wait_recv()
        far_fwd_r.append(go(remote(gathered.at[4, rows], gathered.at[5, rows], right)))
        far_fwd_l.append(go(remote(gathered.at[4, rows], gathered.at[6, rows], left)))

    def forward_far_opp(i):
        lower = pl.ds(i * piece, piece // 2)
        upper = pl.ds(i * piece + piece // 2, piece // 2)
        far_fwd_r[i].wait_recv()
        far_opp.append(go(remote(gathered.at[5, lower], gathered.at[7, lower], right)))
        far_fwd_l[i].wait_recv()
        far_opp.append(go(remote(gathered.at[6, upper], gathered.at[7, upper], left)))

    from_l1.wait_recv()
    opp1 = go(remote(gathered.at[1, first], gathered.at[3, first], right))
    from_r2.wait_recv()
    opp2 = go(remote(gathered.at[2, second], gathered.at[3, second], left))
    forward_far(0)
    momentum_pre(3)
    momentum_pre(4)
    for w in w_copies:
        w.wait_recv()
    mine = w_rows.at[pl.ds(1, 7), share]
    w_x = [go(remote(mine, mine, p)) for p in x_peers]
    from_l2.wait_recv()
    process(1)
    from_r1.wait_recv()
    process(2)
    forward_far(1)
    momentum_pre(5)
    momentum_pre(6)
    forward_far(2)
    opp1.wait_recv()
    opp2.wait_recv()
    process(3)
    momentum_pre(7)
    forward_far_opp(0)
    forward_far(3)
    forward_far_opp(1)
    forward_far(4)
    process(4)
    for w in w_x:
        w.wait_recv()
    w_core = []
    for v in range(4):
        block = w_rows.at[pl.ds(1, 7), 2 * v + c]
        w_core.append(go(remote(block, block, sibling)))
    own_rows = pl.ds(pl.multiple_of(shard[0] * COLS, COLS), COLS)
    w_rows[0] = w_v[own_rows, :].reshape(8, 96, WIDTH)
    forward_far_opp(2)
    forward_far_opp(3)
    forward_far_opp(4)
    process(5)
    process(6)
    for copy in far_opp:
        copy.wait_recv()
    process(7)

    h = hidden[...]
    sig = jax.nn.sigmoid(h)
    act[0] = (cot_ref[...].astype(F32) * sig * (1.0 + h * (1.0 - sig))).astype(BF16)
    act_far = go(remote(act.at[0], act.at[4], far))

    inv = 1.0 / math.sqrt(TOK)
    lower_half = D // SPAN * KEEP // 2

    def code(base):
        def chunk(j, carry):
            rows = pl.ds(pl.multiple_of(base + j * CHUNK, CHUNK), CHUNK)
            grad = jnp.dot(low_t[rows, :], act[0], preferred_element_type=F32)
            own[rows, :] = (low_pre[rows, :] + grad * inv).astype(BF16)
            return carry
        lax.fori_loop(0, lower_half // CHUNK, chunk, 0)

    code((1 - c) * lower_half)
    theirs = pl.ds(pl.multiple_of((1 - c) * lower_half, lower_half), lower_half)
    mine_rows = pl.ds(pl.multiple_of(c * lower_half, lower_half), lower_half)
    red_core = go(remote(own.at[theirs], from_core, sibling))
    act_l = go(remote(act.at[0], act.at[1], right))
    act_r = go(remote(act.at[0], act.at[2], left))
    act_o = go(remote(act.at[0], act.at[3], opp))
    code(c * lower_half)

    mom_copies = []

    def momentum_post(slot):
        def chunk(j, carry):
            rows = pl.ds(pl.multiple_of(shard[slot] * COLS + j * CHUNK, CHUNK), CHUNK)
            t_rows = pl.ds(pl.multiple_of(slot * COLS + j * CHUNK, CHUNK), CHUNK)
            grad = jnp.dot(high_t[t_rows, :], act[0], preferred_element_type=F32)
            mom_v[rows, :] = mom_v[rows, :] + grad * inv
            return carry
        lax.fori_loop(0, COLS // CHUNK, chunk, 0)
        rows = pl.ds(pl.multiple_of(shard[slot] * COLS, COLS), COLS)
        copy = pltpu.make_async_copy(mom_v.at[rows], mom_out.at[rows], local.at[4 + slot])
        copy.start()
        mom_copies.append(copy)

    momentum_post(0)
    red_core.wait_recv()
    part_x[...] = (
        own[mine_rows, :].astype(F32) + from_core[...].astype(F32)
    ).astype(BF16).reshape(4, CODED, WIDTH)
    red_x = [
        go(remote(part_x.at[v], from_x.at[i], p)) for i, (v, p) in enumerate(zip(xs, x_peers))
    ]
    momentum_post(1)
    momentum_post(2)
    momentum_post(3)
    for copy in red_x:
        copy.wait_recv()
    summed = part_x[x].astype(F32)
    for i in range(3):
        summed = summed + from_x[i].astype(F32)
    part_z[...] = summed.astype(BF16).reshape(4, 48, WIDTH)
    red_z = [
        go(remote(part_z.at[v], from_z.at[i], p)) for i, (v, p) in enumerate(zip(zs, z_peers))
    ]
    act_far.wait_recv()
    act_fl = go(remote(act.at[4], act.at[5], right))
    act_fr = go(remote(act.at[4], act.at[6], left))
    act_fo = go(remote(act.at[4], act.at[7], opp))
    momentum_post(4)
    momentum_post(5)
    for copy in red_z:
        copy.wait_recv()
    summed = part_z[zl].astype(F32)
    for i in range(3):
        summed = summed + from_z[i].astype(F32)
    total[c, x, zl] = summed.astype(BF16)
    spread_z = [go(remote(total.at[c, x, zl], total.at[c, x, zl], p)) for p in z_peers]
    momentum_post(6)
    momentum_post(7)
    for copy in spread_z:
        copy.wait_recv()
    spread_x = [go(remote(total.at[c, x], total.at[c, x], p)) for p in x_peers]

    for copy in w_core + [act_l, act_r, act_o, act_fl, act_fr, act_fo]:
        copy.wait_recv()

    def input_grad(j, carry):
        rows = pl.ds(pl.multiple_of(j * 64, 64), 64)
        acc = jnp.zeros((64, COLS), F32)
        for s in range(8):
            acc = acc + lax.dot_general(
                act[s, rows, :], w_rows[s].reshape(COLS, WIDTH),
                (((1,), (1,)), ((), ())), preferred_element_type=F32,
            )
        grad_out[rows, :] = acc.astype(BF16)
        return carry

    lax.fori_loop(0, TOK // 64, input_grad, 0)

    for copy in spread_x:
        copy.wait_recv()
    spread_core = go(remote(total.at[c], total.at[c], sibling))
    spread_core.wait_recv()
    tot_copies = []
    for s in range(8):
        src = total.at[s // 4, s % 4]
        dst = tot_out.at[shard[s]]
        copy = pltpu.make_async_copy(src, dst, local.at[12 + s])
        copy.start()
        tot_copies.append(copy)
    for copy in mom_copies + tot_copies:
        copy.wait()
    for copy in outgoing:
        copy.wait_send()


def decode_kernel(scale, total_ref, decoder_ref, out_ref):
    for j in range(COLS // CHUNK):
        out_ref[pl.ds(j * CHUNK, CHUNK), :] = scale * jnp.dot(
            decoder_ref[...], total_ref[0, pl.ds(j * SPAN, SPAN), :],
            preferred_element_type=F32,
        )


def per_device(tokens, cotangent, weights, momentum):
    replicas = lax.axis_size("replica")
    coder_c = jnp.asarray(coder(), F32).astype(BF16)
    decoder_c = jnp.asarray(decoder(), F32).astype(BF16)
    vmem = pl.BlockSpec(memory_space=pltpu.VMEM)
    hbm = pl.BlockSpec(memory_space=pl.ANY)
    copies = 80
    input_grad, momentum_out, total = pl.pallas_call(
        step_kernel,
        out_shape=(
            jax.ShapeDtypeStruct((TOK, COLS), BF16),
            jax.ShapeDtypeStruct((D, WIDTH), F32),
            jax.ShapeDtypeStruct((8, 4, 48, WIDTH), BF16),
        ),
        in_specs=[hbm, vmem, hbm, hbm, vmem],
        out_specs=(vmem, hbm, hbm),
        scratch_shapes=[
            pltpu.VMEM((8, TOK, COLS), BF16),
            pltpu.VMEM((D, WIDTH), BF16),
            pltpu.VMEM((D, WIDTH), F32),
            pltpu.VMEM((D, TOK), BF16),
            pltpu.VMEM((8 * CODED, TOK), BF16),
            pltpu.VMEM((8 * CODED, WIDTH), F32),
            pltpu.VMEM((TOK, WIDTH), F32),
            pltpu.VMEM((8, TOK, WIDTH), BF16),
            pltpu.VMEM((8, 8, 96, WIDTH), BF16),
            pltpu.VMEM((8 * CODED, WIDTH), BF16),
            pltpu.VMEM((4 * CODED, WIDTH), BF16),
            pltpu.VMEM((3, CODED, WIDTH), BF16),
            pltpu.VMEM((3, 48, WIDTH), BF16),
            pltpu.VMEM((4, CODED, WIDTH), BF16),
            pltpu.VMEM((4, 48, WIDTH), BF16),
            pltpu.VMEM((2, 4, 4, 48, WIDTH), BF16),
            pltpu.SemaphoreType.DMA((copies,)),
            pltpu.SemaphoreType.DMA((copies,)),
            pltpu.SemaphoreType.DMA((20,)),
        ],
        compiler_params=pltpu.CompilerParams(
            collective_id=0, has_side_effects=True, vmem_limit_bytes=56 << 20
        ),
        name="step",
    )(tokens, cotangent, weights, momentum[0], coder_c)
    total = total.reshape(8, CODED, WIDTH)
    update = pl.pallas_call(
        lambda *refs: decode_kernel(1.0 / math.sqrt(replicas), *refs),
        grid=(8,),
        out_shape=jax.ShapeDtypeStruct((D, WIDTH), F32),
        in_specs=[
            pl.BlockSpec((1, CODED, WIDTH), lambda i: (i, 0, 0)),
            pl.BlockSpec((CHUNK, SPAN), lambda i: (0, 0)),
        ],
        out_specs=pl.BlockSpec((COLS, WIDTH), lambda i: (i, 0)),
        name="decode",
    )(total, decoder_c)
    return input_grad, momentum_out[None], update


def solution(mesh):
    in_specs = (
        P("replica", "tensor"),
        P("replica", "tensor"),
        P(None, "tensor"),
        P("replica", None, "tensor"),
    )
    out_specs = (P("replica", "tensor"), P("replica", None, "tensor"), P(None, "tensor"))
    return jax.shard_map(
        per_device, mesh=mesh, in_specs=in_specs, out_specs=out_specs, check_vma=False
    )
```

time: 342 us -> 91.8 us (0.27)
  waiting for transfers between devices: 288 us -> 0 us
  Pallas kernels: 0 us -> 87.2 us
  matrix products: 25.7 us -> 0 us
  between operations: 13.8 us -> 0.65 us
  other arithmetic: 6.65 us -> 0 us
  local copies, waits for them, and re-layouts: 7.1 us -> 3.51 us
    all_gather x2 -> x0, waiting for transfers between devices: 172 us -> none  [the longest x1 102 us: per_device(): rows_full = lax.all_gather(tokens, 'tensor', axis=1, tiled=True)]
    reduce_scatter x1 -> x0, waiting for transfers between devices: 115 us -> none  [per_device(): lax.psum_scatter(partial_terms.astype(jnp.bfloat16), 'tensor', scatter_di...]
    pallas_call x0 -> x2, Pallas kernels: none -> 87.2 us  [the longest x1 81.4 us: per_device(): pl.pallas_call(step_kernel, out_shape=(jax.ShapeDtypeStruct((TOK, COLS),...]
    dot_general x6 -> x0, matrix products: 25.7 us -> none  [the longest x1 5.57 us: per_device(): jnp.einsum('kj,ckf->cjf', table, coeffs, precision=lax.Precision.HIGHEST)]
    reduce_sum x1 -> x0, other arithmetic: 6.63 us -> none  [per_device(): jnp.sum(lax.all_gather(sent[None], 'replica', axis=0, tiled=True).astype(...]
    add x1 -> x0, local copies, waits for them, and re-layouts: 3.54 us -> none  [per_device(): moment_new = decay_rate * momentum[0] + grad_w]
  transfers between devices with their start and end apart: 3 -> 0, of which waited for: 3 -> 0; matrix products, arithmetic and copies ran while one was open for 7% -> 0% of each run, Pallas kernels for 0% -> 0%
where the time goes in v1:
time: 91.8 us; the launch traced here: 91.4 us
  Pallas kernels  87.2 us (95%)
  local copies, waits for them, and re-layouts  3.51 us (4%)
    pallas_call x1, Pallas kernels, per_device(): pl.pallas_call(step_kernel, out_shape=(jax.ShapeDtypeStruct((TOK, COLS),...  81.4 us
    pallas_call x1, Pallas kernels, per_device(): pl.pallas_call(lambda *refs: decode_kernel(1.0 / math.sqrt(replicas), *re...  5.81 us
    unnamed x4, local copies, waits for them, and re-layouts  3.51 us

profile of v1, /device:TPU:1, one launch (start us, length us, event | category | flops | bytes accessed | tf_op | source)
XLA Modules:
  0.0 91.4 jit_solution(1358249161507009142)
XLA Ops:
  0.6 81.4 %step.1 = (bf16[320,768]{1,0:T(8,128)(2,1)}, f32[6144,128]{1,0:T(8,128)}, bf16[8,4,48,128]{3,2,1,0:T(8,128)(2,1)}) custom-call(bf16[320,768]{1,0:T(8,128)(2,1)} %tok_h.1, bf16[320,128]{1,0:T(8,128)(2,1)} %cot_ref.1, bf16[6144,128]{1,0:T(8,128)(2,1)} %w_h.1, f32[6144,128]{1,0:T(8,128)} %bitcast.4, bf16[320,256]{1,0:T(8,128)(2,1)} %constant.7.coder_ref), custom_call_target="tpu_custom_call" | custom-call | tf_op jit(solution)/shard_map/step/pallas_call | solution.py:346
  82.0 0.0 copy-start
  82.0 5.8 %decode.1 = f32[6144,128]{1,0:T(8,128)} custom-call(bf16[8,192,128]{2,1,0:T(8,128)(2,1)} %bitcast.5, bf16[256,64]{1,0:T(8,128)(2,1)} %constant.8.refs_1_), custom_call_target="tpu_custom_call" | custom-call | tf_op jit(solution)/shard_map/decode/pallas_call | solution.py:382
  87.9 1.8 %copy.11 = bf16[320,768]{1,0:T(8,128)(2,1)} copy(bf16[320,768]{1,0:T(8,128)(2,1)} %get-tuple-element.12) | data formatting | bytes 983040
  89.7 0.0 copy-done
  89.7 1.7 %copy.12 = f32[1,6144,128]{2,1,0:T(8,128)} copy(f32[1,6144,128]{2,1,0:T(8,128)S(1)} %bitcast.3) | data formatting | bytes 6291456
Async XLA Ops:
  82.0 7.7 %copy-start = (f32[6144,128]{1,0:T(8,128)S(1)}, f32[6144,128]{1,0:T(8,128)}, u32[]{:S(2)}) copy-start(f32[6144,128]{1,0:T(8,128)} %get-tuple-element.7) | copy-start | bytes 9437188

commit v2 on v1

v2 whole, which is shorter than its diff:
```python
import math

import jax
import jax.numpy as jnp
import numpy as np
from jax import lax
from jax.experimental import pallas as pl
from jax.experimental.pallas import tpu as pltpu
from jax.sharding import PartitionSpec as P

SPAN = 64
KEEP = 16
D = 6144
TOK = 320
COLS = 768
WIDTH = 128
CODED = 192
CHUNK = 256
DECAY = 0.9
MESH = pl.DeviceIdType.MESH
F32 = jnp.float32
BF16 = jnp.bfloat16


def cosine_table():
    order = np.arange(KEEP, dtype=np.float64)[:, None]
    place = np.arange(SPAN, dtype=np.float64)[None, :]
    table = np.cos(np.pi * (place + 0.5) * order / SPAN) * math.sqrt(2.0 / SPAN)
    return np.where(order == 0, table * math.sqrt(0.5), table)


def coder():
    table = cosine_table()
    four = np.eye(CHUNK // SPAN)
    rest = np.kron(four, np.eye(SPAN) - table.T @ table)
    return np.concatenate([rest, np.kron(four, table)], axis=0)


def decoder():
    return np.kron(np.eye(CHUNK // SPAN), cosine_table().T)


def position():
    t = lax.axis_index("tensor")
    r = lax.axis_index("replica")
    return r // 8, t % 4, t // 4, (r // 2) % 4, r % 2


def device(x, y, zh, zl, c):
    return (zh * 4 + y, (x * 4 + zl) * 2 + c)


def step_kernel(
    tok_h, cot_ref, w_h, mom_h, coder_ref,
    grad_out, mom_out, tot_out,
    gathered, w_v, mom_v, high_t, low_t, low_pre, hidden, act, w_rows,
    to_core, from_core, part_x, kept_x, from_x, part_z, to_z, from_z,
    send, recv, local,
):
    x, y, zh, zl, c = position()
    yr, yl, yo = (y + 1) % 4, (y + 3) % 4, (y + 2) % 4
    zo = 1 - zh
    right, left, opp = device(x, yr, zh, zl, c), device(x, yl, zh, zl, c), device(x, yo, zh, zl, c)
    far = device(x, y, zo, zl, c)
    far_l, far_r, far_o = device(x, yl, zo, zl, c), device(x, yr, zo, zl, c), device(x, yo, zo, zl, c)
    sibling = device(x, y, zh, zl, 1 - c)
    xs = [(x + d) % 4 for d in (1, 2, 3)]
    zs = [(zl + d) % 4 for d in (1, 2, 3)]
    x_peers = [device(v, y, zh, zl, c) for v in xs]
    z_peers = [device(x, y, zh, v, c) for v in zs]
    shard = [zh * 4 + v for v in (y, yl, yr, yo)] + [zo * 4 + v for v in (y, yl, yr, yo)]
    tensor_peers = [None, left, right, opp, far, far_l, far_r, far_o]

    counter = iter(range(1000))

    def remote(src, dst, target):
        k = next(counter)
        return pltpu.make_async_remote_copy(
            src_ref=src, dst_ref=dst, send_sem=send.at[k], recv_sem=recv.at[k],
            device_id=target, device_id_type=MESH,
        )

    barrier = pltpu.get_barrier_semaphore()
    partners = tensor_peers[1:] + [sibling] + x_peers + z_peers
    for p in partners:
        pl.semaphore_signal(barrier, inc=1, device_id=p, device_id_type=MESH)

    tok_in = pltpu.make_async_copy(tok_h, gathered.at[0], local.at[0])
    tok_in.start()
    w_in = pltpu.make_async_copy(w_h, w_v, local.at[1])
    w_in.start()
    mom_in = pltpu.make_async_copy(mom_h, mom_v, local.at[2])
    mom_in.start()
    hidden[...] = jnp.zeros_like(hidden)

    pl.semaphore_wait(barrier, len(partners))

    outgoing = []

    def go(copy):
        copy.start()
        outgoing.append(copy)
        return copy

    def process(slot):
        rows = pl.ds(pl.multiple_of(shard[slot] * COLS, COLS), COLS)
        hidden[...] += jnp.dot(gathered[slot], w_v[rows, :], preferred_element_type=F32)
        for j in range(COLS // CHUNK):
            coded = lax.dot_general(
                coder_ref[...], gathered[slot, :, j * CHUNK:(j + 1) * CHUNK],
                (((1,), (1,)), ((), ())), preferred_element_type=F32,
            ).astype(BF16)
            high_t[pl.ds(slot * COLS + j * CHUNK, CHUNK), :] = coded[:CHUNK]
            low_t[pl.ds(slot * CODED + j * SPAN, SPAN), :] = coded[CHUNK:]

    def momentum_pre(slot):
        def chunk(j, carry):
            rows = pl.ds(pl.multiple_of(shard[slot] * COLS + j * CHUNK, CHUNK), CHUNK)
            slot_rows = pl.ds(pl.multiple_of(slot * COLS + j * CHUNK, CHUNK), CHUNK)
            coded = DECAY * jnp.dot(
                coder_ref[...], mom_v[rows, :].astype(BF16), preferred_element_type=F32
            )
            mom_out[slot_rows, :] = coded[:CHUNK]
            low_pre[pl.ds(pl.multiple_of(slot * CODED + j * SPAN, SPAN), SPAN), :] = coded[CHUNK:]
            return carry
        lax.fori_loop(0, COLS // CHUNK, chunk, 0)
    half = TOK // 2
    piece = 64
    pieces = TOK // piece
    first = pl.ds(0, half)
    second = pl.ds(half, half)
    far_in, far_fwd_r, far_fwd_l, far_opp = [], [], [], []

    def send_far(i):
        rows = pl.ds(i * piece, piece)
        far_in.append(go(remote(tok_h.at[rows], gathered.at[4, rows], far)))

    def forward_far(i):
        rows = pl.ds(i * piece, piece)
        far_in[i].wait_recv()
        if i + 2 < pieces:
            send_far(i + 2)
        far_fwd_r.append(go(remote(gathered.at[4, rows], gathered.at[5, rows], right)))
        far_fwd_l.append(go(remote(gathered.at[4, rows], gathered.at[6, rows], left)))

    def forward_far_opp(i):
        lower = pl.ds(i * piece, piece // 2)
        upper = pl.ds(i * piece + piece // 2, piece // 2)
        far_fwd_r[i].wait_recv()
        far_opp.append(go(remote(gathered.at[5, lower], gathered.at[7, lower], right)))
        far_fwd_l[i].wait_recv()
        far_opp.append(go(remote(gathered.at[6, upper], gathered.at[7, upper], left)))

    send_far(0)
    from_l1 = go(remote(tok_h.at[first], gathered.at[1, first], right))
    from_r2 = go(remote(tok_h.at[second], gathered.at[2, second], left))
    send_far(1)
    from_l2 = go(remote(tok_h.at[second], gathered.at[1, second], right))
    from_r1 = go(remote(tok_h.at[first], gathered.at[2, first], left))

    w_in.wait()
    tok_in.wait()
    process(0)
    mom_in.wait()
    momentum_pre(0)
    momentum_pre(1)
    forward_far(0)
    momentum_pre(2)
    momentum_pre(3)
    forward_far(1)
    momentum_pre(4)
    from_l1.wait_recv()
    opp1 = go(remote(gathered.at[1, first], gathered.at[3, first], right))
    from_r2.wait_recv()
    opp2 = go(remote(gathered.at[2, second], gathered.at[3, second], left))
    momentum_pre(5)
    forward_far(2)
    from_l2.wait_recv()
    process(1)
    forward_far_opp(0)
    from_r1.wait_recv()
    process(2)
    forward_far(3)
    momentum_pre(6)
    forward_far_opp(1)
    momentum_pre(7)
    forward_far(4)
    w_copies = []
    mirror = [0, 2, 1, 3, 4, 6, 5, 7]
    share = 2 * x + c
    for s in range(1, 8):
        rows = pl.ds(pl.multiple_of(shard[s] * COLS + share * 96, 32), 96)
        w_copies.append(
            go(remote(w_v.at[rows], w_rows.at[mirror[s], share], tensor_peers[s]))
        )
    forward_far_opp(2)
    process(4)
    forward_far_opp(3)
    opp1.wait_recv()
    opp2.wait_recv()
    process(3)
    forward_far_opp(4)
    process(5)
    process(6)
    for w in w_copies:
        w.wait_recv()
    mine = w_rows.at[pl.ds(1, 7), share]
    w_x = [go(remote(mine, mine, p)) for p in x_peers]
    for copy in far_opp:
        copy.wait_recv()
    process(7)

    h = hidden[...]
    sig = jax.nn.sigmoid(h)
    act[0] = (cot_ref[...].astype(F32) * sig * (1.0 + h * (1.0 - sig))).astype(BF16)
    act_far = go(remote(act.at[0], act.at[4], far))

    inv = 1.0 / math.sqrt(TOK)

    def code(slot):
        rows = pl.ds(pl.multiple_of(slot * CODED, CODED), CODED)
        grad = jnp.dot(low_t[rows, :], act[0], preferred_element_type=F32)
        return low_pre[rows, :] + grad * inv

    def momentum_post(slot):
        def chunk(j, carry):
            rows = pl.ds(pl.multiple_of(slot * COLS + j * CHUNK, CHUNK), CHUNK)
            grad = jnp.dot(high_t[rows, :], act[0], preferred_element_type=F32)
            mom_out[rows, :] = mom_out[rows, :] + grad * inv
            return carry
        lax.fori_loop(0, COLS // CHUNK, chunk, 0)

    order = [xs[1], xs[0], xs[2], x]
    red_core = []
    for i, v in enumerate(order):
        to_core[i] = code((1 - c) * 4 + v).astype(BF16)
        red_core.append(go(remote(to_core.at[i], from_core.at[i], sibling)))
    red_x = []
    peers_of = [x_peers[1], x_peers[0], x_peers[2]]
    for i, v in enumerate(order):
        mine_q = code(c * 4 + v)
        red_core[i].wait_recv()
        both = mine_q + from_core[i].astype(F32)
        if i < 3:
            part_x[i] = both.astype(BF16)
            red_x.append(go(remote(part_x.at[i], from_x.at[i], peers_of[i])))
        else:
            kept_x[...] = both
    act_l = go(remote(act.at[0], act.at[1], right))
    act_r = go(remote(act.at[0], act.at[2], left))
    act_o = go(remote(act.at[0], act.at[3], opp))
    for w in w_x:
        w.wait_recv()
    w_core = []
    for v in range(4):
        block = w_rows.at[pl.ds(1, 7), 2 * v + c]
        w_core.append(go(remote(block, block, sibling)))
    momentum_post(0)
    momentum_post(1)
    momentum_post(2)
    for copy in red_x:
        copy.wait_recv()
    part_z[...] = (
        kept_x[...] + from_x[0].astype(F32) + from_x[1].astype(F32) + from_x[2].astype(F32)
    ).reshape(4, 48, WIDTH)
    to_z[...] = part_z[...].astype(BF16)
    red_z = [
        go(remote(to_z.at[v], from_z.at[i], p)) for i, (v, p) in enumerate(zip(zs, z_peers))
    ]
    act_far.wait_recv()
    act_fl = go(remote(act.at[4], act.at[5], right))
    act_fr = go(remote(act.at[4], act.at[6], left))
    act_fo = go(remote(act.at[4], act.at[7], opp))
    momentum_post(3)
    momentum_post(4)
    for copy in red_z:
        copy.wait_recv()
    tot_out[c, x, zl] = (
        part_z[zl] + from_z[0].astype(F32) + from_z[1].astype(F32) + from_z[2].astype(F32)
    ).astype(BF16)
    piece_ref = tot_out.at[c, x, zl]
    spread_z = [go(remote(piece_ref, piece_ref, p)) for p in z_peers]
    spread_x = [[go(remote(piece_ref, piece_ref, p)) for p in x_peers]]
    own_rows = pl.ds(pl.multiple_of(shard[0] * COLS, COLS), COLS)
    w_rows[0] = w_v[own_rows, :].reshape(8, 96, WIDTH)
    momentum_post(5)
    for i in range(3):
        spread_z[i].wait_recv()
        got = tot_out.at[c, x, zs[2 - i]]
        spread_x.append([go(remote(got, got, p)) for p in x_peers])
    quarter = tot_out.at[c, x]
    spread_core = [go(remote(quarter, quarter, sibling))]
    momentum_post(6)
    momentum_post(7)
    for copy in w_core + [act_l, act_r, act_o, act_fl, act_fr, act_fo]:
        copy.wait_recv()

    def input_grad(j, carry):
        rows = pl.ds(pl.multiple_of(j * 64, 64), 64)
        acc = jnp.zeros((64, COLS), F32)
        for s in range(8):
            acc = acc + lax.dot_general(
                act[s, rows, :], w_rows[s].reshape(COLS, WIDTH),
                (((1,), (1,)), ((), ())), preferred_element_type=F32,
            )
        grad_out[rows, :] = acc.astype(BF16)
        return carry

    lax.fori_loop(0, TOK // 64, input_grad, 0)

    for i in range(3):
        for copies in spread_x:
            copies[i].wait_recv()
        got = tot_out.at[c, xs[2 - i]]
        spread_core.append(go(remote(got, got, sibling)))
    for copy in spread_core:
        copy.wait_recv()
    for copy in outgoing:
        copy.wait_send()


def write_kernel(scale, grad_ref, mom_ref, total_ref, decoder_ref, grad_out, mom_out, upd_out, update, sems):
    x, y, zh, zl, c = position()
    zo = 1 - zh
    ys = (y, (y + 3) % 4, (y + 1) % 4, (y + 2) % 4)
    shard = [zh * 4 + v for v in ys] + [zo * 4 + v for v in ys]
    copies = []

    def put(src, dst):
        copies.append(pltpu.make_async_copy(src, dst, sems.at[len(copies)]))
        copies[-1].start()

    for s in range(8):
        rows = pl.ds(pl.multiple_of(shard[s] * COLS, COLS), COLS)
        put(mom_ref.at[pl.ds(s * COLS, COLS)], mom_out.at[0, rows])
    put(grad_ref, grad_out)
    for s in range(8):
        coded = total_ref[s // 4, s % 4].reshape(CODED, WIDTH)
        for j in range(COLS // CHUNK):
            update[pl.ds(s * COLS + j * CHUNK, CHUNK), :] = scale * jnp.dot(
                decoder_ref[...], coded[j * SPAN:(j + 1) * SPAN], preferred_element_type=F32
            )
        rows = pl.ds(pl.multiple_of(shard[s] * COLS, COLS), COLS)
        put(update.at[pl.ds(s * COLS, COLS)], upd_out.at[rows])
    for copy in copies:
        copy.wait()


def per_device(tokens, cotangent, weights, momentum):
    replicas = lax.axis_size("replica")
    coder_c = jnp.asarray(coder(), F32).astype(BF16)
    decoder_c = jnp.asarray(decoder(), F32).astype(BF16)
    vmem = pl.BlockSpec(memory_space=pltpu.VMEM)
    hbm = pl.BlockSpec(memory_space=pltpu.HBM)
    copies = 100
    input_grad, momentum_out, total = pl.pallas_call(
        step_kernel,
        out_shape=(
            pltpu.VMEM((TOK, COLS), BF16),
            pltpu.VMEM((D, WIDTH), F32),
            pltpu.VMEM((2, 4, 4, 48, WIDTH), BF16),
        ),
        in_specs=[hbm, vmem, hbm, hbm, vmem],
        out_specs=(vmem, vmem, vmem),
        scratch_shapes=[
            pltpu.VMEM((8, TOK, COLS), BF16),
            pltpu.VMEM((D, WIDTH), BF16),
            pltpu.VMEM((D, WIDTH), F32),
            pltpu.VMEM((D, TOK), BF16),
            pltpu.VMEM((8 * CODED, TOK), BF16),
            pltpu.VMEM((8 * CODED, WIDTH), F32),
            pltpu.VMEM((TOK, WIDTH), F32),
            pltpu.VMEM((8, TOK, WIDTH), BF16),
            pltpu.VMEM((8, 8, 96, WIDTH), BF16),
            pltpu.VMEM((4, CODED, WIDTH), BF16),
            pltpu.VMEM((4, CODED, WIDTH), BF16),
            pltpu.VMEM((3, CODED, WIDTH), BF16),
            pltpu.VMEM((CODED, WIDTH), F32),
            pltpu.VMEM((3, CODED, WIDTH), BF16),
            pltpu.VMEM((4, 48, WIDTH), F32),
            pltpu.VMEM((4, 48, WIDTH), BF16),
            pltpu.VMEM((3, 48, WIDTH), BF16),
            pltpu.SemaphoreType.DMA((copies,)),
            pltpu.SemaphoreType.DMA((copies,)),
            pltpu.SemaphoreType.DMA((3,)),
        ],
        compiler_params=pltpu.CompilerParams(
            collective_id=0, has_side_effects=True, vmem_limit_bytes=52 << 20
        ),
        name="step",
    )(tokens, cotangent, weights, momentum[0], coder_c)
    return pl.pallas_call(
        lambda *refs: write_kernel(1.0 / math.sqrt(replicas), *refs),
        out_shape=(
            jax.ShapeDtypeStruct((TOK, COLS), BF16),
            jax.ShapeDtypeStruct((1, D, WIDTH), F32),
            jax.ShapeDtypeStruct((D, WIDTH), F32),
        ),
        in_specs=[vmem] * 4,
        out_specs=(hbm, hbm, hbm),
        scratch_shapes=[pltpu.VMEM((D, WIDTH), F32), pltpu.SemaphoreType.DMA((17,))],
        compiler_params=pltpu.CompilerParams(vmem_limit_bytes=16 << 20),
        name="write",
    )(input_grad, momentum_out, total, decoder_c)


def solution(mesh):
    in_specs = (
        P("replica", "tensor"),
        P("replica", "tensor"),
        P(None, "tensor"),
        P("replica", None, "tensor"),
    )
    out_specs = (P("replica", "tensor"), P("replica", None, "tensor"), P(None, "tensor"))
    return jax.shard_map(
        per_device, mesh=mesh, in_specs=in_specs, out_specs=out_specs, check_vma=False
    )
```

time: 91.8 us -> 76.4 us (0.83)
  Pallas kernels: 87.2 us -> 75.7 us
  local copies, waits for them, and re-layouts: 3.51 us -> 0.01 us
    pallas_call x2, Pallas kernels: 87.2 us -> 75.7 us  [the longest x1 72.7 us: per_device(): pl.pallas_call(step_kernel, out_shape=(pltpu.VMEM((TOK, COLS), BF16), plt...]
    unnamed x4 -> x2, local copies, waits for them, and re-layouts: 3.51 us -> 0.01 us
where the time goes in v2:
time: 76.4 us; the launch traced here: 76.3 us
  Pallas kernels  75.7 us (99%)
    pallas_call x1, Pallas kernels, per_device(): pl.pallas_call(step_kernel, out_shape=(pltpu.VMEM((TOK, COLS), BF16), plt...  72.7 us
    pallas_call x1, Pallas kernels, per_device(): pl.pallas_call(lambda *refs: write_kernel(1.0 / math.sqrt(replicas), *ref...  2.96 us

profile of v2, /device:TPU:1, one launch (start us, length us, event | category | flops | bytes accessed | tf_op | source)
XLA Modules:
  0.0 76.3 jit_solution(735660429867647424)
XLA Ops:
  0.6 0.0 copy-start
  0.6 72.7 %step.1 = (bf16[320,768]{1,0:T(8,128)(2,1)S(1)}, f32[6144,128]{1,0:T(8,128)S(1)}, bf16[2,4,4,48,128]{4,3,2,1,0:T(8,128)(2,1)S(1)}) custom-call(bf16[320,768]{1,0:T(8,128)(2,1)} %tok_h.1, bf16[320,128]{1,0:T(8,128)(2,1)} %cot_ref.1, bf16[6144,128]{1,0:T(8,128)(2,1)} %w_h.1, f32[6144,128]{1,0:T(8,128)} %bitcast.1, bf16[320,256]{1,0:T(8,128)(2,1)} %constant.7.coder_ref), custom_call_target="tpu_custom_call" | custom-call | tf_op jit(solution)/shard_map/step/pallas_call | solution.py:356
  73.4 0.0 copy-done
  73.4 3.0 %write.1 = (bf16[320,768]{1,0:T(8,128)(2,1)}, f32[1,6144,128]{2,1,0:T(8,128)}, f32[6144,128]{1,0:T(8,128)}) custom-call(bf16[320,768]{1,0:T(8,128)(2,1)S(1)} %get-tuple-element.6.refs_0_, f32[6144,128]{1,0:T(8,128)S(1)} %get-tuple-element.7.refs_1_, bf16[2,4,4,48,128]{4,3,2,1,0:T(8,128)(2,1)S(1)} %get-tuple-element.8.refs_2_, bf16[256,64]{1,0:T(8,128)(2,1)S(1)} %copy-done), custom_call_target="tpu_custom_call" | custom-call | tf_op jit(solution)/shard_map/write/pallas_call | solution.py:392
Async XLA Ops:
  0.6 72.7 %copy-start = (bf16[256,64]{1,0:T(8,128)(2,1)S(1)}, bf16[256,64]{1,0:T(8,128)(2,1)}, u32[]{:S(2)}) copy-start(bf16[256,64]{1,0:T(8,128)(2,1)} %constant.8.refs_3_) | copy-start | bytes 98308

commit v3 on v2

v3 whole, which is shorter than its diff:
```python
import math

import jax
import jax.numpy as jnp
import numpy as np
from jax import lax
from jax.experimental import pallas as pl
from jax.experimental.pallas import tpu as pltpu
from jax.sharding import PartitionSpec as P

SPAN = 64
KEEP = 16
D = 6144
TOK = 320
COLS = 768
WIDTH = 128
CODED = 192
CHUNK = 256
FIRST = 256
DECAY = 0.9
MESH = pl.DeviceIdType.MESH
F32 = jnp.float32
BF16 = jnp.bfloat16


def cosine_basis():
    order = np.arange(SPAN, dtype=np.float64)[:, None]
    place = np.arange(SPAN, dtype=np.float64)[None, :]
    table = np.cos(np.pi * (place + 0.5) * order / SPAN) * math.sqrt(2.0 / SPAN)
    return np.where(order == 0, table * math.sqrt(0.5), table)


def cosine_table():
    return cosine_basis()[:KEEP]


def shard_basis():
    blocks = np.kron(np.eye(COLS // SPAN), cosine_basis().T).reshape(COLS, COLS // SPAN, SPAN)
    kept = blocks[:, :, :KEEP].reshape(COLS, -1)
    others = blocks[:, :, KEEP:].reshape(COLS, -1)
    return np.concatenate([kept, others], axis=1)


def coder():
    table = cosine_table()
    four = np.eye(CHUNK // SPAN)
    rest = np.kron(four, np.eye(SPAN) - table.T @ table)
    return np.concatenate([rest, np.kron(four, table)], axis=0)


def decoder():
    return np.kron(np.eye(CHUNK // SPAN), cosine_table().T)


def position():
    t = lax.axis_index("tensor")
    r = lax.axis_index("replica")
    return r // 8, t % 4, t // 4, (r // 2) % 4, r % 2


def device(x, y, zh, zl, c):
    return (zh * 4 + y, (x * 4 + zl) * 2 + c)


def step_kernel(
    tok_h, cot_h, w_h, mom_h, coder_h, basis_h, rest_h, pick_h,
    grad_out, mom_out, tot_out,
    coder_ref, basis_ref, rest_ref, pick_ref, cot_ref,
    gathered, spectra_own, spectra, w_v, w_far, w_rows, mom_v, high_t, low_t, low_pre,
    hidden, hidden_far, give_far, take_far, act,
    to_core, from_core, part_x, kept_x, from_x, part_z, to_z, from_z,
    send, recv, local,
):
    x, y, zh, zl, c = position()
    yr, yl, yo = (y + 1) % 4, (y + 3) % 4, (y + 2) % 4
    zo = 1 - zh
    right, left, opp = device(x, yr, zh, zl, c), device(x, yl, zh, zl, c), device(x, yo, zh, zl, c)
    far = device(x, y, zo, zl, c)
    sibling = device(x, y, zh, zl, 1 - c)
    xs = [(x + d) % 4 for d in (1, 2, 3)]
    zs = [(zl + d) % 4 for d in (1, 2, 3)]
    x_peers = [device(v, y, zh, zl, c) for v in xs]
    z_peers = [device(x, y, zh, v, c) for v in zs]
    places = (y, yl, yr, yo)
    shard = [zh * 4 + v for v in places] + [zo * 4 + v for v in places]
    counter = iter(range(1000))

    def remote(src, dst, target):
        k = next(counter)
        return pltpu.make_async_remote_copy(
            src_ref=src, dst_ref=dst, send_sem=send.at[k], recv_sem=recv.at[k],
            device_id=target, device_id_type=MESH,
        )

    barrier = pltpu.get_barrier_semaphore()
    partners = [right, left, opp, far, sibling] + x_peers + z_peers
    for p in partners:
        pl.semaphore_signal(barrier, inc=1, device_id=p, device_id_type=MESH)

    def fetch(src, dst, k):
        copy = pltpu.make_async_copy(src, dst, local.at[k])
        copy.start()
        return copy

    tok_in = fetch(tok_h, gathered.at[0], 0)
    basis_in = fetch(basis_h, basis_ref, 1)
    coder_in = fetch(coder_h, coder_ref, 2)
    mom_in = fetch(mom_h, mom_v, 3)
    w_in = fetch(w_h, w_v, 4)
    rest_in = fetch(rest_h, rest_ref, 5)
    pick_in = fetch(pick_h, pick_ref, 6)
    cot_in = fetch(cot_h, cot_ref, 7)

    outgoing = []

    def go(copy):
        copy.start()
        outgoing.append(copy)
        return copy

    def spectrum(j):
        cols = slice(j * CHUNK, (j + 1) * CHUNK)
        spectra_own[:, cols] = jnp.dot(
            gathered[0], basis_ref[:, cols], preferred_element_type=F32
        ).astype(BF16)

    def code_tokens(slot):
        for j in range(COLS // CHUNK):
            coded = lax.dot_general(
                coder_ref[...], gathered[slot, :, j * CHUNK:(j + 1) * CHUNK],
                (((1,), (1,)), ((), ())), preferred_element_type=F32,
            ).astype(BF16)
            high_t[pl.ds(slot * COLS + j * CHUNK, CHUNK), :] = coded[:CHUNK]
            low_t[pl.ds(slot * CODED + j * SPAN, SPAN), :] = coded[CHUNK:]

    def low_far(i):
        low_t[pl.ds((4 + i) * CODED, CODED), :] = lax.dot_general(
            pick_ref[...], spectra[i, :, :FIRST],
            (((1,), (1,)), ((), ())), preferred_element_type=F32,
        ).astype(BF16)

    def high_far(i):
        for j in range(COLS // CHUNK):
            high_t[pl.ds((4 + i) * COLS + j * CHUNK, CHUNK), :] = lax.dot_general(
                rest_ref[j * CHUNK:(j + 1) * CHUNK, :], spectra[i],
                (((1,), (1,)), ((), ())), preferred_element_type=F32,
            ).astype(BF16)

    def add_hidden(slot):
        rows = gathered[slot]
        hidden[...] += jnp.dot(
            rows, w_v[shard[slot]].reshape(COLS, WIDTH), preferred_element_type=F32
        )
        hidden_far[...] += jnp.dot(
            rows, w_far[places[slot]].reshape(COLS, WIDTH), preferred_element_type=F32
        )

    def momentum_pre(slot):
        for j in range(COLS // CHUNK):
            rows = pl.ds(pl.multiple_of(shard[slot] * COLS + j * CHUNK, CHUNK), CHUNK)
            coded = DECAY * jnp.dot(
                coder_ref[...], mom_v[rows, :].astype(BF16), preferred_element_type=F32
            )
            mom_out[pl.ds(slot * COLS + j * CHUNK, CHUNK), :] = coded[:CHUNK]
            low_pre[pl.ds(slot * CODED + j * SPAN, SPAN), :] = coded[CHUNK:]

    hidden[...] = jnp.zeros_like(hidden)
    hidden_far[...] = jnp.zeros_like(hidden_far)
    tok_in.wait()
    basis_in.wait()
    for j in range(COLS // CHUNK):
        spectrum(j)

    pl.semaphore_wait(barrier, len(partners))

    half = TOK // 2
    first, second = pl.ds(0, half), pl.ds(half, half)
    piece = 64
    pieces = TOK // piece
    lows, highs = pl.ds(0, FIRST), pl.ds(FIRST, COLS - FIRST)

    w_z = go(remote(w_h.at[pl.ds(zo * 4, 4), x, c], w_far.at[:, x, c], far))
    from_l1 = go(remote(tok_h.at[first], gathered.at[1, first], right))
    from_r2 = go(remote(tok_h.at[second], gathered.at[2, second], left))
    from_l2 = go(remote(tok_h.at[second], gathered.at[1, second], right))
    from_r1 = go(remote(tok_h.at[first], gathered.at[2, first], left))
    coder_in.wait()
    code_tokens(0)
    mom_in.wait()
    for s in range(4):
        momentum_pre(s)
    low_z = go(remote(spectra_own.at[:, lows], spectra.at[0, :, lows], far))
    high_z, high_r, high_l, high_o = [], [], [], []

    def send_high():
        rows = pl.ds(len(high_z) * piece, piece)
        high_z.append(go(remote(spectra_own.at[rows, highs], spectra.at[0, rows, highs], far)))

    def forward_high(i):
        rows = pl.ds(i * piece, piece)
        high_z[i].wait_recv()
        high_r.append(go(remote(spectra.at[0, rows, highs], spectra.at[1, rows, highs], right)))
        high_l.append(go(remote(spectra.at[0, rows, highs], spectra.at[2, rows, highs], left)))

    def forward_high_opp(i):
        lower = pl.ds(i * piece, piece // 2)
        upper = pl.ds(i * piece + piece // 2, piece // 2)
        high_r[i].wait_recv()
        high_o.append(go(remote(spectra.at[1, lower, highs], spectra.at[3, lower, highs], right)))
        high_l[i].wait_recv()
        high_o.append(go(remote(spectra.at[2, upper, highs], spectra.at[3, upper, highs], left)))

    send_high()
    send_high()
    send_high()
    for s in range(4, 8):
        momentum_pre(s)
    w_z.wait_recv()
    w_x = [go(remote(w_far.at[:, x, c], w_far.at[:, x, c], p)) for p in x_peers]
    from_l1.wait_recv()
    opp1 = go(remote(gathered.at[1, first], gathered.at[3, first], right))
    from_r2.wait_recv()
    opp2 = go(remote(gathered.at[2, second], gathered.at[3, second], left))
    send_high()
    for copy in w_x:
        copy.wait_recv()
    w_core = go(remote(w_far.at[:, :, c], w_far.at[:, :, c], sibling))
    from_l2.wait_recv()
    code_tokens(1)
    from_r1.wait_recv()
    code_tokens(2)
    w_in.wait()
    w_core.wait_recv()
    add_hidden(0)
    add_hidden(1)
    add_hidden(2)
    opp1.wait_recv()
    opp2.wait_recv()
    low_z.wait_recv()
    low_r = go(remote(spectra.at[0, :, lows], spectra.at[1, :, lows], right))
    low_l = go(remote(spectra.at[0, :, lows], spectra.at[2, :, lows], left))
    add_hidden(3)
    give_far[...] = hidden_far[...].astype(BF16)
    hidden_z = go(remote(give_far, take_far, far))
    send_high()
    code_tokens(3)
    pick_in.wait()
    low_far(0)
    mirror = [0, 2, 1, 3]
    near = [None, left, right, opp]
    rows_y = []

    low_r.wait_recv()
    low_o1 = go(remote(spectra.at[1, first, lows], spectra.at[3, first, lows], right))
    low_l.wait_recv()
    low_o2 = go(remote(spectra.at[2, second, lows], spectra.at[3, second, lows], left))
    for s in range(1, 4):
        rows_y.append(
            go(remote(w_v.at[shard[s], x, c], w_rows.at[mirror[s] - 1, x, c], near[s]))
        )
        rows_y.append(
            go(remote(w_far.at[places[s], x, c], w_rows.at[mirror[s] + 2, x, c], near[s]))
        )
    low_far(1)
    low_far(2)
    cot_in.wait()
    hidden_z.wait_recv()

    h = hidden[...] + take_far[...].astype(F32)
    sig = jax.nn.sigmoid(h)
    act[0] = (cot_ref[...].astype(F32) * sig * (1.0 + h * (1.0 - sig))).astype(BF16)
    act_z = go(remote(act.at[0], act.at[4], far))

    inv = 1.0 / math.sqrt(TOK)

    def code(slot):
        rows = pl.ds(pl.multiple_of(slot * CODED, CODED), CODED)
        grad = jnp.dot(low_t[rows, :], act[0], preferred_element_type=F32)
        return low_pre[rows, :] + grad * inv

    def momentum_post(slot):
        rows = pl.ds(slot * COLS, COLS)
        grad = jnp.dot(high_t[rows, :], act[0], preferred_element_type=F32)
        mom_out[rows, :] = mom_out[rows, :] + grad * inv

    low_o1.wait_recv()
    low_o2.wait_recv()
    for i in range(4):
        forward_high(i)
    low_far(3)
    order = [xs[1], xs[0], xs[2], x]
    peers_of = [x_peers[1], x_peers[0], x_peers[2]]
    red_core = []
    for i, v in enumerate(order):
        to_core[i] = code((1 - c) * 4 + v).astype(BF16)
        red_core.append(go(remote(to_core.at[i], from_core.at[i], sibling)))
    red_x = []
    for i, v in enumerate(order):
        own = code(c * 4 + v)
        red_core[i].wait_recv()
        both = own + from_core[i].astype(F32)
        if i < 3:
            part_x[i] = both.astype(BF16)
            red_x.append(go(remote(part_x.at[i], from_x.at[i], peers_of[i])))
        else:
            kept_x[...] = both
    act_l = go(remote(act.at[0], act.at[1], right))
    act_r = go(remote(act.at[0], act.at[2], left))
    act_o = go(remote(act.at[0], act.at[3], opp))
    forward_high(4)
    for s in range(4):
        momentum_post(s)
    for copy in red_x:
        copy.wait_recv()
    part_z[...] = (
        kept_x[...] + from_x[0].astype(F32) + from_x[1].astype(F32) + from_x[2].astype(F32)
    ).reshape(4, 48, WIDTH)
    to_z[...] = part_z[...].astype(BF16)
    red_z = [
        go(remote(to_z.at[v], from_z.at[i], p)) for i, (v, p) in enumerate(zip(zs, z_peers))
    ]
    for copy in rows_y:
        copy.wait_recv()
    share = w_rows.at[:, x, c]
    rows_x = [go(remote(share, share, p)) for p in x_peers]
    act_z.wait_recv()
    act_fl = go(remote(act.at[4], act.at[5], right))
    act_fr = go(remote(act.at[4], act.at[6], left))
    act_fo = go(remote(act.at[4], act.at[7], opp))
    rest_in.wait()
    high_far(0)
    for copy in red_z:
        copy.wait_recv()
    tot_out[c, x, zl] = (
        part_z[zl] + from_z[0].astype(F32) + from_z[1].astype(F32) + from_z[2].astype(F32)
    ).astype(BF16)
    piece_ref = tot_out.at[c, x, zl]
    spread_z = [go(remote(piece_ref, piece_ref, p)) for p in z_peers]
    spread_x = [[go(remote(piece_ref, piece_ref, p)) for p in x_peers]]
    momentum_post(4)
    for i in range(2):
        forward_high_opp(i)
    for i in range(3):
        spread_z[i].wait_recv()
        got = tot_out.at[c, x, zs[2 - i]]
        spread_x.append([go(remote(got, got, p)) for p in x_peers])
    quarter = tot_out.at[c, x]
    spread_core = [go(remote(quarter, quarter, sibling))]
    for i in range(2, 5):
        forward_high_opp(i)
    for copy in rows_x:
        copy.wait_recv()
    rows_core = go(remote(w_rows.at[:, :, c], w_rows.at[:, :, c], sibling))
    high_far(1)
    momentum_post(5)
    for i in range(3):
        for copies in spread_x:
            copies[i].wait_recv()
        got = tot_out.at[c, xs[2 - i]]
        spread_core.append(go(remote(got, got, sibling)))
    high_far(2)
    momentum_post(6)
    for copy in high_o:
        copy.wait_recv()
    high_far(3)
    momentum_post(7)
    for copy in [rows_core, act_l, act_r, act_o, act_fl, act_fr, act_fo]:
        copy.wait_recv()

    def weight_rows(s):
        if s == 0:
            return w_v[shard[0]].reshape(COLS, WIDTH)
        if s == 4:
            return w_far[y].reshape(COLS, WIDTH)
        return w_rows[s - 1 if s < 4 else s - 2].reshape(COLS, WIDTH)

    for j in range(COLS // CHUNK):
        cols = slice(j * CHUNK, (j + 1) * CHUNK)
        acc = jnp.zeros((TOK, CHUNK), F32)
        for s in range(8):
            acc = acc + lax.dot_general(
                act[s], weight_rows(s)[cols], (((1,), (1,)), ((), ())),
                preferred_element_type=F32,
            )
        grad_out[:, cols] = acc.astype(BF16)

    for copy in spread_core:
        copy.wait_recv()
    for copy in outgoing:
        copy.wait_send()


def write_kernel(scale, grad_ref, mom_ref, total_ref, decoder_ref, grad_out, mom_out, upd_out, update, sems):
    x, y, zh, zl, c = position()
    zo = 1 - zh
    ys = (y, (y + 3) % 4, (y + 1) % 4, (y + 2) % 4)
    shard = [zh * 4 + v for v in ys] + [zo * 4 + v for v in ys]
    copies = []

    def put(src, dst):
        copies.append(pltpu.make_async_copy(src, dst, sems.at[len(copies)]))
        copies[-1].start()

    for s in range(8):
        rows = pl.ds(pl.multiple_of(shard[s] * COLS, COLS), COLS)
        put(mom_ref.at[pl.ds(s * COLS, COLS)], mom_out.at[0, rows])
    put(grad_ref, grad_out)
    for s in range(8):
        coded = total_ref[s // 4, s % 4].reshape(CODED, WIDTH)
        for j in range(COLS // CHUNK):
            update[pl.ds(s * COLS + j * CHUNK, CHUNK), :] = scale * jnp.dot(
                decoder_ref[...], coded[j * SPAN:(j + 1) * SPAN], preferred_element_type=F32
            )
        rows = pl.ds(pl.multiple_of(shard[s] * COLS, COLS), COLS)
        put(update.at[pl.ds(s * COLS, COLS)], upd_out.at[rows])
    for copy in copies:
        copy.wait()


def per_device(tokens, cotangent, weights, momentum):
    replicas = lax.axis_size("replica")

    def constant(values):
        return jnp.asarray(values, F32).astype(BF16)

    basis = shard_basis()
    rest = np.where(np.arange(COLS)[None, :] < CODED, 0.0, basis)
    pick = np.eye(CODED, FIRST)
    decoder_c = constant(decoder())
    vmem = pl.BlockSpec(memory_space=pltpu.VMEM)
    hbm = pl.BlockSpec(memory_space=pltpu.HBM)
    copies = 120
    split = (4, 2, 96, WIDTH)
    input_grad, momentum_out, total = pl.pallas_call(
        step_kernel,
        out_shape=(
            pltpu.VMEM((TOK, COLS), BF16),
            pltpu.VMEM((D, WIDTH), F32),
            pltpu.VMEM((2, 4, 4, 48, WIDTH), BF16),
        ),
        in_specs=[hbm] * 8,
        out_specs=(vmem, vmem, vmem),
        scratch_shapes=[
            pltpu.VMEM((CHUNK + SPAN, CHUNK), BF16),
            pltpu.VMEM((COLS, COLS), BF16),
            pltpu.VMEM((COLS, COLS), BF16),
            pltpu.VMEM((CODED, FIRST), BF16),
            pltpu.VMEM((TOK, WIDTH), BF16),
            pltpu.VMEM((4, TOK, COLS), BF16),
            pltpu.VMEM((TOK, COLS), BF16),
            pltpu.VMEM((4, TOK, COLS), BF16),
            pltpu.VMEM((8,) + split, BF16),
            pltpu.VMEM((4,) + split, BF16),
            pltpu.VMEM((6,) + split, BF16),
            pltpu.VMEM((D, WIDTH), F32),
            pltpu.VMEM((D, TOK), BF16),
            pltpu.VMEM((8 * CODED, TOK), BF16),
            pltpu.VMEM((8 * CODED, WIDTH), F32),
            pltpu.VMEM((TOK, WIDTH), F32),
            pltpu.VMEM((TOK, WIDTH), F32),
            pltpu.VMEM((TOK, WIDTH), BF16),
            pltpu.VMEM((TOK, WIDTH), BF16),
            pltpu.VMEM((8, TOK, WIDTH), BF16),
            pltpu.VMEM((4, CODED, WIDTH), BF16),
            pltpu.VMEM((4, CODED, WIDTH), BF16),
            pltpu.VMEM((3, CODED, WIDTH), BF16),
            pltpu.VMEM((CODED, WIDTH), F32),
            pltpu.VMEM((3, CODED, WIDTH), BF16),
            pltpu.VMEM((4, 48, WIDTH), F32),
            pltpu.VMEM((4, 48, WIDTH), BF16),
            pltpu.VMEM((3, 48, WIDTH), BF16),
            pltpu.SemaphoreType.DMA((copies,)),
            pltpu.SemaphoreType.DMA((copies,)),
            pltpu.SemaphoreType.DMA((8,)),
        ],
        compiler_params=pltpu.CompilerParams(
            collective_id=0, has_side_effects=True, vmem_limit_bytes=52 << 20
        ),
        name="step",
    )(
        tokens, cotangent, weights.reshape((8,) + split), momentum[0],
        constant(coder()), constant(basis), constant(rest), constant(pick),
    )
    return pl.pallas_call(
        lambda *refs: write_kernel(1.0 / math.sqrt(replicas), *refs),
        out_shape=(
            jax.ShapeDtypeStruct((TOK, COLS), BF16),
            jax.ShapeDtypeStruct((1, D, WIDTH), F32),
            jax.ShapeDtypeStruct((D, WIDTH), F32),
        ),
        in_specs=[vmem] * 4,
        out_specs=(hbm, hbm, hbm),
        scratch_shapes=[pltpu.VMEM((D, WIDTH), F32), pltpu.SemaphoreType.DMA((17,))],
        compiler_params=pltpu.CompilerParams(vmem_limit_bytes=16 << 20),
        name="write",
    )(input_grad, momentum_out, total, decoder_c)


def solution(mesh):
    in_specs = (
        P("replica", "tensor"),
        P("replica", "tensor"),
        P(None, "tensor"),
        P("replica", None, "tensor"),
    )
    out_specs = (P("replica", "tensor"), P("replica", None, "tensor"), P(None, "tensor"))
    return jax.shard_map(
        per_device, mesh=mesh, in_specs=in_specs, out_specs=out_specs, check_vma=False
    )
```

time: 76.4 us -> 67.4 us (0.88)
  Pallas kernels: 75.7 us -> 66.7 us
    pallas_call x1, Pallas kernels: 72.7 us -> 63.7 us  [per_device(): pl.pallas_call(step_kernel, out_shape=(pltpu.VMEM((TOK, COLS), BF16), plt...]
where the time goes in v3:
time: 67.4 us; the launch traced here: 67.3 us
  Pallas kernels  66.7 us (99%)
    pallas_call x1, Pallas kernels, per_device(): pl.pallas_call(step_kernel, out_shape=(pltpu.VMEM((TOK, COLS), BF16), plt...  63.7 us
    pallas_call x1, Pallas kernels, per_device(): pl.pallas_call(lambda *refs: write_kernel(1.0 / math.sqrt(replicas), *ref...  2.96 us

profile of v3, /device:TPU:1, one launch (start us, length us, event | category | flops | bytes accessed | tf_op | source)
XLA Modules:
  0.0 67.3 jit_solution(2205815590400879492)
XLA Ops:
  0.6 0.0 copy-start
  0.6 63.7 %step.1 = (bf16[320,768]{1,0:T(8,128)(2,1)S(1)}, f32[6144,128]{1,0:T(8,128)S(1)}, bf16[2,4,4,48,128]{4,3,2,1,0:T(8,128)(2,1)S(1)}) custom-call(bf16[320,768]{1,0:T(8,128)(2,1)} %tok_h.1, bf16[320,128]{1,0:T(8,128)(2,1)} %cot_h.1, bf16[8,4,2,96,128]{4,3,2,1,0:T(8,128)(2,1)} %bitcast.3, f32[6144,128]{1,0:T(8,128)} %bitcast.2, ...), custom_call_target="tpu_custom_call" | custom-call | tf_op jit(solution)/shard_map/step/pallas_call | solution.py:434
  64.3 0.0 copy-done
  64.4 3.0 %write.1 = (bf16[320,768]{1,0:T(8,128)(2,1)}, f32[1,6144,128]{2,1,0:T(8,128)}, f32[6144,128]{1,0:T(8,128)}) custom-call(bf16[320,768]{1,0:T(8,128)(2,1)S(1)} %get-tuple-element.6.refs_0_, f32[6144,128]{1,0:T(8,128)S(1)} %get-tuple-element.7.refs_1_, bf16[2,4,4,48,128]{4,3,2,1,0:T(8,128)(2,1)S(1)} %get-tuple-element.8.refs_2_, bf16[256,64]{1,0:T(8,128)(2,1)S(1)} %copy-done), custom_call_target="tpu_custom_call" | custom-call | tf_op jit(solution)/shard_map/write/pallas_call | solution.py:484
Async XLA Ops:
  0.6 63.7 %copy-start = (bf16[256,64]{1,0:T(8,128)(2,1)S(1)}, bf16[256,64]{1,0:T(8,128)(2,1)}, u32[]{:S(2)}) copy-start(bf16[256,64]{1,0:T(8,128)(2,1)} %constant.20.refs_3_) | copy-start | bytes 98308

commit v4 on v3

--- a/solution.py
+++ b/solution.py
@@ -66,8 +66,8 @@
     tok_h, cot_h, w_h, mom_h, coder_h, basis_h, rest_h, pick_h,
     grad_out, mom_out, tot_out,
     coder_ref, basis_ref, rest_ref, pick_ref, cot_ref,
-    gathered, spectra_own, spectra, w_v, w_far, w_rows, mom_v, high_t, low_t, low_pre,
-    hidden, hidden_far, give_far, take_far, act,
+    gathered, spectra_own, spectra, w_pair, w_rows, mom_v, high_t, low_t, low_pre,
+    hidden, give_far, take_far, act,
     to_core, from_core, part_x, kept_x, from_x, part_z, to_z, from_z,
     send, recv, local,
 ):
@@ -106,7 +106,8 @@
     basis_in = fetch(basis_h, basis_ref, 1)
     coder_in = fetch(coder_h, coder_ref, 2)
     mom_in = fetch(mom_h, mom_v, 3)
-    w_in = fetch(w_h, w_v, 4)
+    nears, fars = pl.ds(0, WIDTH), pl.ds(WIDTH, WIDTH)
+    w_in = fetch(w_h.at[pl.ds(zh * 4, 4)], w_pair.at[:, :, :, :, nears], 4)
     rest_in = fetch(rest_h, rest_ref, 5)
     pick_in = fetch(pick_h, pick_ref, 6)
     cot_in = fetch(cot_h, cot_ref, 7)
@@ -146,13 +147,10 @@
                 (((1,), (1,)), ((), ())), preferred_element_type=F32,
             ).astype(BF16)
 
-    def add_hidden(slot):
-        rows = gathered[slot]
-        hidden[...] += jnp.dot(
-            rows, w_v[shard[slot]].reshape(COLS, WIDTH), preferred_element_type=F32
-        )
-        hidden_far[...] += jnp.dot(
-            rows, w_far[places[slot]].reshape(COLS, WIDTH), preferred_element_type=F32
+    def add_hidden(slot, rows):
+        hidden[rows, :] += jnp.dot(
+            gathered[slot, rows, :], w_pair[places[slot]].reshape(COLS, 2 * WIDTH),
+            preferred_element_type=F32,
         )
 
     def momentum_pre(slot):
@@ -165,7 +163,6 @@
             low_pre[pl.ds(slot * CODED + j * SPAN, SPAN), :] = coded[CHUNK:]
 
     hidden[...] = jnp.zeros_like(hidden)
-    hidden_far[...] = jnp.zeros_like(hidden_far)
     tok_in.wait()
     basis_in.wait()
     for j in range(COLS // CHUNK):
@@ -174,16 +171,16 @@
     pl.semaphore_wait(barrier, len(partners))
 
     half = TOK // 2
-    first, second = pl.ds(0, half), pl.ds(half, half)
+    halves = [pl.ds(0, half), pl.ds(half, half)]
+    upper = [pl.ds(0, half // 2), pl.ds(half, half // 2)]
+    lower = [pl.ds(half // 2, half // 2), pl.ds(half + half // 2, half // 2)]
     piece = 64
     pieces = TOK // piece
     lows, highs = pl.ds(0, FIRST), pl.ds(FIRST, COLS - FIRST)
 
-    w_z = go(remote(w_h.at[pl.ds(zo * 4, 4), x, c], w_far.at[:, x, c], far))
-    from_l1 = go(remote(tok_h.at[first], gathered.at[1, first], right))
-    from_r2 = go(remote(tok_h.at[second], gathered.at[2, second], left))
-    from_l2 = go(remote(tok_h.at[second], gathered.at[1, second], right))
-    from_r1 = go(remote(tok_h.at[first], gathered.at[2, first], left))
+    w_z = go(remote(w_h.at[pl.ds(zo * 4, 4), x, c], w_pair.at[:, x, c, :, fars], far))
+    from_l = [go(remote(tok_h.at[halves[0]], gathered.at[1, halves[0]], right))]
+    from_r = [go(remote(tok_h.at[halves[0]], gathered.at[2, halves[0]], left))]
     coder_in.wait()
     code_tokens(0)
     mom_in.wait()
@@ -203,89 +200,107 @@
         high_l.append(go(remote(spectra.at[0, rows, highs], spectra.at[2, rows, highs], left)))
 
     def forward_high_opp(i):
-        lower = pl.ds(i * piece, piece // 2)
-        upper = pl.ds(i * piece + piece // 2, piece // 2)
+        one = pl.ds(i * piece, piece // 2)
+        two = pl.ds(i * piece + piece // 2, piece // 2)
         high_r[i].wait_recv()
-        high_o.append(go(remote(spectra.at[1, lower, highs], spectra.at[3, lower, highs], right)))
+        high_o.append(go(remote(spectra.at[1, one, highs], spectra.at[3, one, highs], right)))
         high_l[i].wait_recv()
-        high_o.append(go(remote(spectra.at[2, upper, highs], spectra.at[3, upper, highs], left)))
-
-    send_high()
-    send_high()
+        high_o.append(go(remote(spectra.at[2, two, highs], spectra.at[3, two, highs], left)))
+
     send_high()
     for s in range(4, 8):
         momentum_pre(s)
+    from_l.append(go(remote(tok_h.at[halves[1]], gathered.at[1, halves[1]], right)))
+    from_r.append(go(remote(tok_h.at[halves[1]], gathered.at[2, halves[1]], left)))
     w_z.wait_recv()
-    w_x = [go(remote(w_far.at[:, x, c], w_far.at[:, x, c], p)) for p in x_peers]
-    from_l1.wait_recv()
-    opp1 = go(remote(gathered.at[1, first], gathered.at[3, first], right))
-    from_r2.wait_recv()
-    opp2 = go(remote(gathered.at[2, second], gathered.at[3, second], left))
+    share = w_pair.at[:, x, c, :, fars]
+    w_x = [go(remote(share, share, p)) for p in x_peers]
+    from_o = []
+
+    def forward_tokens(i):
+        from_l[i].wait_recv()
+        from_o.append(go(remote(gathered.at[1, upper[i]], gathered.at[3, upper[i]], right)))
+        from_r[i].wait_recv()
+        from_o.append(go(remote(gathered.at[2, lower[i]], gathered.at[3, lower[i]], left)))
+
+    forward_tokens(0)
+    send_high()
     send_high()
     for copy in w_x:
         copy.wait_recv()
-    w_core = go(remote(w_far.at[:, :, c], w_far.at[:, :, c], sibling))
-    from_l2.wait_recv()
+    share = w_pair.at[:, :, c, :, fars]
+    w_core = go(remote(share, share, sibling))
+    forward_tokens(1)
     code_tokens(1)
-    from_r1.wait_recv()
     code_tokens(2)
     w_in.wait()
     w_core.wait_recv()
-    add_hidden(0)
-    add_hidden(1)
-    add_hidden(2)
-    opp1.wait_recv()
-    opp2.wait_recv()
+    for s in range(3):
+        add_hidden(s, halves[0])
+    from_o[0].wait_recv()
+    from_o[1].wait_recv()
+    add_hidden(3, halves[0])
+    hidden_z = []
+
+    def send_hidden(i):
+        give_far[halves[i], :] = hidden[halves[i], fars].astype(BF16)
+        hidden_z.append(go(remote(give_far.at[halves[i]], take_far.at[halves[i]], far)))
+
+    send_hidden(0)
+    for s in range(3):
+        add_hidden(s, halves[1])
     low_z.wait_recv()
-    low_r = go(remote(spectra.at[0, :, lows], spectra.at[1, :, lows], right))
-    low_l = go(remote(spectra.at[0, :, lows], spectra.at[2, :, lows], left))
-    add_hidden(3)
-    give_far[...] = hidden_far[...].astype(BF16)
-    hidden_z = go(remote(give_far, take_far, far))
+    from_o[2].wait_recv()
+    from_o[3].wait_recv()
+    low_r = [go(remote(spectra.at[0, halves[0], lows], spectra.at[1, halves[0], lows], right))]
+    low_l = [go(remote(spectra.at[0, halves[0], lows], spectra.at[2, halves[0], lows], left))]
+    add_hidden(3, halves[1])
+    send_hidden(1)
+    low_r.append(go(remote(spectra.at[0, halves[1], lows], spectra.at[1, halves[1], lows], right)))
+    low_l.append(go(remote(spectra.at[0, halves[1], lows], spectra.at[2, halves[1], lows], left)))
+    send_high()
     send_high()
     code_tokens(3)
     pick_in.wait()
     low_far(0)
+    low_o = []
+    for i in range(2):
+        low_r[i].wait_recv()
+        low_o.append(go(remote(spectra.at[1, upper[i], lows], spectra.at[3, upper[i], lows], right)))
+        low_l[i].wait_recv()
+        low_o.append(go(remote(spectra.at[2, lower[i], lows], spectra.at[3, lower[i], lows], left)))
     mirror = [0, 2, 1, 3]
     near = [None, left, right, opp]
-    rows_y = []
-
-    low_r.wait_recv()
-    low_o1 = go(remote(spectra.at[1, first, lows], spectra.at[3, first, lows], right))
-    low_l.wait_recv()
-    low_o2 = go(remote(spectra.at[2, second, lows], spectra.at[3, second, lows], left))
-    for s in range(1, 4):
-        rows_y.append(
-            go(remote(w_v.at[shard[s], x, c], w_rows.at[mirror[s] - 1, x, c], near[s]))
-        )
-        rows_y.append(
-            go(remote(w_far.at[places[s], x, c], w_rows.at[mirror[s] + 2, x, c], near[s]))
-        )
+    rows_y = [
+        go(remote(w_pair.at[places[s], x, c], w_rows.at[mirror[s] - 1, x, c], near[s]))
+        for s in range(1, 4)
+    ]
     low_far(1)
     low_far(2)
     cot_in.wait()
-    hidden_z.wait_recv()
-
-    h = hidden[...] + take_far[...].astype(F32)
+    for copy in hidden_z:
+        copy.wait_recv()
+
+    h = hidden[:, nears] + take_far[...].astype(F32)
     sig = jax.nn.sigmoid(h)
-    act[0] = (cot_ref[...].astype(F32) * sig * (1.0 + h * (1.0 - sig))).astype(BF16)
-    act_z = go(remote(act.at[0], act.at[4], far))
+    act[0, :, nears] = (cot_ref[...].astype(F32) * sig * (1.0 + h * (1.0 - sig))).astype(BF16)
+    act_z = go(remote(act.at[0, :, nears], act.at[0, :, fars], far))
 
     inv = 1.0 / math.sqrt(TOK)
 
     def code(slot):
         rows = pl.ds(pl.multiple_of(slot * CODED, CODED), CODED)
-        grad = jnp.dot(low_t[rows, :], act[0], preferred_element_type=F32)
+        grad = jnp.dot(low_t[rows, :], act[0, :, nears], preferred_element_type=F32)
         return low_pre[rows, :] + grad * inv
 
     def momentum_post(slot):
         rows = pl.ds(slot * COLS, COLS)
-        grad = jnp.dot(high_t[rows, :], act[0], preferred_element_type=F32)
+        grad = jnp.dot(high_t[rows, :], act[0, :, nears], preferred_element_type=F32)
         mom_out[rows, :] = mom_out[rows, :] + grad * inv
 
-    low_o1.wait_recv()
-    low_o2.wait_recv()
-    for i in range(4):
+    for copy in low_o:
+        copy.wait_recv()
+    for i in range(3):
         forward_high(i)
     low_far(3)
     order = [xs[1], xs[0], xs[2], x]
@@ -304,12 +319,12 @@
             red_x.append(go(remote(part_x.at[i], from_x.at[i], peers_of[i])))
         else:
             kept_x[...] = both
-    act_l = go(remote(act.at[0], act.at[1], right))
-    act_r = go(remote(act.at[0], act.at[2], left))
-    act_o = go(remote(act.at[0], act.at[3], opp))
-    forward_high(4)
+    act_l = go(remote(act.at[0, :, nears], act.at[1, :, nears], right))
+    act_r = go(remote(act.at[0, :, nears], act.at[2, :, nears], left))
+    act_o = go(remote(act.at[0, :, nears], act.at[3, :, nears], opp))
     for s in range(4):
         momentum_post(s)
+    forward_high(3)
     for copy in red_x:
         copy.wait_recv()
     part_z[...] = (
@@ -323,10 +338,11 @@
         copy.wait_recv()
     share = w_rows.at[:, x, c]
     rows_x = [go(remote(share, share, p)) for p in x_peers]
+    forward_high(4)
     act_z.wait_recv()
-    act_fl = go(remote(act.at[4], act.at[5], right))
-    act_fr = go(remote(act.at[4], act.at[6], left))
-    act_fo = go(remote(act.at[4], act.at[7], opp))
+    act_fl = go(remote(act.at[0, :, fars], act.at[1, :, fars], right))
+    act_fr = go(remote(act.at[0, :, fars], act.at[2, :, fars], left))
+    act_fo = go(remote(act.at[0, :, fars], act.at[3, :, fars], opp))
     rest_in.wait()
     high_far(0)
     for copy in red_z:
@@ -368,16 +384,13 @@
         copy.wait_recv()
 
     def weight_rows(s):
-        if s == 0:
-            return w_v[shard[0]].reshape(COLS, WIDTH)
-        if s == 4:
-            return w_far[y].reshape(COLS, WIDTH)
-        return w_rows[s - 1 if s < 4 else s - 2].reshape(COLS, WIDTH)
+        block = w_pair[y] if s == 0 else w_rows[s - 1]
+        return block.reshape(COLS, 2 * WIDTH)
 
     for j in range(COLS // CHUNK):
         cols = slice(j * CHUNK, (j + 1) * CHUNK)
         acc = jnp.zeros((TOK, CHUNK), F32)
-        for s in range(8):
+        for s in range(4):
             acc = acc + lax.dot_general(
                 act[s], weight_rows(s)[cols], (((1,), (1,)), ((), ())),
                 preferred_element_type=F32,
@@ -431,6 +444,7 @@
     hbm = pl.BlockSpec(memory_space=pltpu.HBM)
     copies = 120
     split = (4, 2, 96, WIDTH)
+    pair = (4, 2, 96, 2 * WIDTH)
     input_grad, momentum_out, total = pl.pallas_call(
         step_kernel,
         out_shape=(
@@ -449,18 +463,16 @@
             pltpu.VMEM((4, TOK, COLS), BF16),
             pltpu.VMEM((TOK, COLS), BF16),
             pltpu.VMEM((4, TOK, COLS), BF16),
-            pltpu.VMEM((8,) + split, BF16),
-            pltpu.VMEM((4,) + split, BF16),
-            pltpu.VMEM((6,) + split, BF16),
+            pltpu.VMEM((4,) + pair, BF16),
+            pltpu.VMEM((3,) + pair, BF16),
             pltpu.VMEM((D, WIDTH), F32),
             pltpu.VMEM((D, TOK), BF16),
             pltpu.VMEM((8 * CODED, TOK), BF16),
             pltpu.VMEM((8 * CODED, WIDTH), F32),
-            pltpu.VMEM((TOK, WIDTH), F32),
-            pltpu.VMEM((TOK, WIDTH), F32),
+            pltpu.VMEM((TOK, 2 * WIDTH), F32),
             pltpu.VMEM((TOK, WIDTH), BF16),
             pltpu.VMEM((TOK, WIDTH), BF16),
-            pltpu.VMEM((8, TOK, WIDTH), BF16),
+            pltpu.VMEM((4, TOK, 2 * WIDTH), BF16),
             pltpu.VMEM((4, CODED, WIDTH), BF16),
             pltpu.VMEM((4, CODED, WIDTH), BF16),
             pltpu.VMEM((3, CODED, WIDTH), BF16),

time: 67.4 us -> 65.1 us (0.966)
  Pallas kernels: 66.7 us -> 64.3 us
    pallas_call x1, Pallas kernels: 63.7 us -> 61.3 us  [per_device(): pl.pallas_call(step_kernel, out_shape=(pltpu.VMEM((TOK, COLS), BF16), plt...]
where the time goes in v4:
time: 65.1 us; the launch traced here: 64.9 us
  Pallas kernels  64.3 us (99%)
    pallas_call x1, Pallas kernels, per_device(): pl.pallas_call(step_kernel, out_shape=(pltpu.VMEM((TOK, COLS), BF16), plt...  61.3 us
    pallas_call x1, Pallas kernels, per_device(): pl.pallas_call(lambda *refs: write_kernel(1.0 / math.sqrt(replicas), *ref...  2.96 us

profile of v4, /device:TPU:1, one launch (start us, length us, event | category | flops | bytes accessed | tf_op | source)
XLA Modules:
  0.0 64.9 jit_solution(4342075120370110571)
XLA Ops:
  0.6 0.0 copy-start
  0.6 61.3 %step.1 = (bf16[320,768]{1,0:T(8,128)(2,1)S(1)}, f32[6144,128]{1,0:T(8,128)S(1)}, bf16[2,4,4,48,128]{4,3,2,1,0:T(8,128)(2,1)S(1)}) custom-call(bf16[320,768]{1,0:T(8,128)(2,1)} %tok_h.1, bf16[320,128]{1,0:T(8,128)(2,1)} %cot_h.1, bf16[8,4,2,96,128]{4,3,2,1,0:T(8,128)(2,1)} %bitcast.3, f32[6144,128]{1,0:T(8,128)} %bitcast.2, ...), custom_call_target="tpu_custom_call" | custom-call | tf_op jit(solution)/shard_map/step/pallas_call | solution.py:448
  62.0 0.0 copy-done
  62.0 3.0 %write.1 = (bf16[320,768]{1,0:T(8,128)(2,1)}, f32[1,6144,128]{2,1,0:T(8,128)}, f32[6144,128]{1,0:T(8,128)}) custom-call(bf16[320,768]{1,0:T(8,128)(2,1)S(1)} %get-tuple-element.6.refs_0_, f32[6144,128]{1,0:T(8,128)S(1)} %get-tuple-element.7.refs_1_, bf16[2,4,4,48,128]{4,3,2,1,0:T(8,128)(2,1)S(1)} %get-tuple-element.8.refs_2_, bf16[256,64]{1,0:T(8,128)(2,1)S(1)} %copy-done), custom_call_target="tpu_custom_call" | custom-call | tf_op jit(solution)/shard_map/write/pallas_call | solution.py:496
Async XLA Ops:
  0.6 61.3 %copy-start = (bf16[256,64]{1,0:T(8,128)(2,1)S(1)}, bf16[256,64]{1,0:T(8,128)(2,1)}, u32[]{:S(2)}) copy-start(bf16[256,64]{1,0:T(8,128)(2,1)} %constant.20.refs_3_) | copy-start | bytes 98308

commit v5 on v4

--- a/solution.py
+++ b/solution.py
@@ -269,6 +269,7 @@
         low_o.append(go(remote(spectra.at[1, upper[i], lows], spectra.at[3, upper[i], lows], right)))
         low_l[i].wait_recv()
         low_o.append(go(remote(spectra.at[2, lower[i], lows], spectra.at[3, lower[i], lows], left)))
+    forward_high(0)
     mirror = [0, 2, 1, 3]
     near = [None, left, right, opp]
     rows_y = [
@@ -300,8 +301,8 @@
 
     for copy in low_o:
         copy.wait_recv()
-    for i in range(3):
-        forward_high(i)
+    forward_high(1)
+    forward_high(2)
     low_far(3)
     order = [xs[1], xs[0], xs[2], x]
     peers_of = [x_peers[1], x_peers[0], x_peers[2]]
@@ -343,8 +344,6 @@
     act_fl = go(remote(act.at[0, :, fars], act.at[1, :, fars], right))
     act_fr = go(remote(act.at[0, :, fars], act.at[2, :, fars], left))
     act_fo = go(remote(act.at[0, :, fars], act.at[3, :, fars], opp))
-    rest_in.wait()
-    high_far(0)
     for copy in red_z:
         copy.wait_recv()
     tot_out[c, x, zl] = (
@@ -353,6 +352,8 @@
     piece_ref = tot_out.at[c, x, zl]
     spread_z = [go(remote(piece_ref, piece_ref, p)) for p in z_peers]
     spread_x = [[go(remote(piece_ref, piece_ref, p)) for p in x_peers]]
+    rest_in.wait()
+    high_far(0)
     momentum_post(4)
     for i in range(2):
         forward_high_opp(i)

time: 65.1 us -> 65.1 us (level)
  no operation moved by 1% of the time
where the time goes in v5:
time: 65.1 us; the launch traced here: 64.8 us
  Pallas kernels  64.1 us (98%)
    pallas_call x1, Pallas kernels, per_device(): pl.pallas_call(step_kernel, out_shape=(pltpu.VMEM((TOK, COLS), BF16), plt...  61.1 us
    pallas_call x1, Pallas kernels, per_device(): pl.pallas_call(lambda *refs: write_kernel(1.0 / math.sqrt(replicas), *ref...  2.96 us

profile of v5, /device:TPU:1, one launch (start us, length us, event | category | flops | bytes accessed | tf_op | source)
XLA Modules:
  0.0 64.8 jit_solution(6895028083972952733)
XLA Ops:
  0.6 0.0 copy-start
  0.6 61.1 %step.1 = (bf16[320,768]{1,0:T(8,128)(2,1)S(1)}, f32[6144,128]{1,0:T(8,128)S(1)}, bf16[2,4,4,48,128]{4,3,2,1,0:T(8,128)(2,1)S(1)}) custom-call(bf16[320,768]{1,0:T(8,128)(2,1)} %tok_h.1, bf16[320,128]{1,0:T(8,128)(2,1)} %cot_h.1, bf16[8,4,2,96,128]{4,3,2,1,0:T(8,128)(2,1)} %bitcast.3, f32[6144,128]{1,0:T(8,128)} %bitcast.2, ...), custom_call_target="tpu_custom_call" | custom-call | tf_op jit(solution)/shard_map/step/pallas_call | solution.py:449
  61.8 0.0 copy-done
  61.8 3.0 %write.1 = (bf16[320,768]{1,0:T(8,128)(2,1)}, f32[1,6144,128]{2,1,0:T(8,128)}, f32[6144,128]{1,0:T(8,128)}) custom-call(bf16[320,768]{1,0:T(8,128)(2,1)S(1)} %get-tuple-element.6.refs_0_, f32[6144,128]{1,0:T(8,128)S(1)} %get-tuple-element.7.refs_1_, bf16[2,4,4,48,128]{4,3,2,1,0:T(8,128)(2,1)S(1)} %get-tuple-element.8.refs_2_, bf16[256,64]{1,0:T(8,128)(2,1)S(1)} %copy-done), custom_call_target="tpu_custom_call" | custom-call | tf_op jit(solution)/shard_map/write/pallas_call | solution.py:497
Async XLA Ops:
  0.6 61.2 %copy-start = (bf16[256,64]{1,0:T(8,128)(2,1)S(1)}, bf16[256,64]{1,0:T(8,128)(2,1)}, u32[]{:S(2)}) copy-start(bf16[256,64]{1,0:T(8,128)(2,1)} %constant.20.refs_3_) | copy-start | bytes 98308

commit v6 on v5

--- a/solution.py
+++ b/solution.py
@@ -377,10 +377,6 @@
         spread_core.append(go(remote(got, got, sibling)))
     high_far(2)
     momentum_post(6)
-    for copy in high_o:
-        copy.wait_recv()
-    high_far(3)
-    momentum_post(7)
     for copy in [rows_core, act_l, act_r, act_o, act_fl, act_fr, act_fo]:
         copy.wait_recv()
 
@@ -398,6 +394,10 @@
             )
         grad_out[:, cols] = acc.astype(BF16)
 
+    for copy in high_o:
+        copy.wait_recv()
+    high_far(3)
+    momentum_post(7)
     for copy in spread_core:
         copy.wait_recv()
     for copy in outgoing:

time: 65.1 us -> 65.3 us (level); the launches traced: 64.8 us -> 64.1 us
  Pallas kernels: 64.1 us -> 63.4 us
    pallas_call x1, Pallas kernels: 61.1 us -> 60.4 us  [per_device(): pl.pallas_call(step_kernel, out_shape=(pltpu.VMEM((TOK, COLS), BF16), plt...]
where the time goes in v6:
time: 65.3 us; the launch traced here: 64.1 us
  Pallas kernels  63.4 us (97%)
    pallas_call x1, Pallas kernels, per_device(): pl.pallas_call(step_kernel, out_shape=(pltpu.VMEM((TOK, COLS), BF16), plt...  60.4 us
    pallas_call x1, Pallas kernels, per_device(): pl.pallas_call(lambda *refs: write_kernel(1.0 / math.sqrt(replicas), *ref...  2.96 us

profile of v6, /device:TPU:1, one launch (start us, length us, event | category | flops | bytes accessed | tf_op | source)
XLA Modules:
  0.0 64.1 jit_solution(16093638333137289964)
XLA Ops:
  0.6 0.0 copy-start
  0.6 60.4 %step.1 = (bf16[320,768]{1,0:T(8,128)(2,1)S(1)}, f32[6144,128]{1,0:T(8,128)S(1)}, bf16[2,4,4,48,128]{4,3,2,1,0:T(8,128)(2,1)S(1)}) custom-call(bf16[320,768]{1,0:T(8,128)(2,1)} %tok_h.1, bf16[320,128]{1,0:T(8,128)(2,1)} %cot_h.1, bf16[8,4,2,96,128]{4,3,2,1,0:T(8,128)(2,1)} %bitcast.3, f32[6144,128]{1,0:T(8,128)} %bitcast.2, ...), custom_call_target="tpu_custom_call" | custom-call | tf_op jit(solution)/shard_map/step/pallas_call | solution.py:449
  61.1 0.0 copy-done
  61.1 3.0 %write.1 = (bf16[320,768]{1,0:T(8,128)(2,1)}, f32[1,6144,128]{2,1,0:T(8,128)}, f32[6144,128]{1,0:T(8,128)}) custom-call(bf16[320,768]{1,0:T(8,128)(2,1)S(1)} %get-tuple-element.6.refs_0_, f32[6144,128]{1,0:T(8,128)S(1)} %get-tuple-element.7.refs_1_, bf16[2,4,4,48,128]{4,3,2,1,0:T(8,128)(2,1)S(1)} %get-tuple-element.8.refs_2_, bf16[256,64]{1,0:T(8,128)(2,1)S(1)} %copy-done), custom_call_target="tpu_custom_call" | custom-call | tf_op jit(solution)/shard_map/write/pallas_call | solution.py:497
Async XLA Ops:
  0.6 60.5 %copy-start = (bf16[256,64]{1,0:T(8,128)(2,1)S(1)}, bf16[256,64]{1,0:T(8,128)(2,1)}, u32[]{:S(2)}) copy-start(bf16[256,64]{1,0:T(8,128)(2,1)} %constant.20.refs_3_) | copy-start | bytes 98308
